TPU v7x, 32 devices: a whole 2x2x4 slice. The times are simulated.
32 devices in a mesh: ctx: 8 (over y, x, core), tp: 4 (over z).
Axes of the slice: x: 2, y: 2, z: 4, core: 2. Of those that a mesh axis runs over, the one named last changes fastest.
Arguments:
- ctx_heads: bfloat16 [8192, 4096], P('ctx', 'tp'), may hold values from -6 to 6
- out_weight: bfloat16 [4096, 4096], P('ctx', 'tp'), may hold values from -0.09375 to 0.09375
- hidden_in: bfloat16 [8192, 4096], P(('ctx', 'tp')), may hold values from -54 to 54
- norm_gain: float32 [4096], replicated, may hold values from 0.5 to 1.5
- expert_ids: int32 [8192, 2], P(('ctx', 'tp')), may hold values from 0 to 15, all different within a row; in each aligned block of 256 rows (0 to 255, 256 to 511, ...) at most 48 rows name the same one
- route_weights: float32 [8192, 2], P(('ctx', 'tp')), may hold values from 0.02 to 0.4
- w_gate: bfloat16 [32, 4096, 384], P(('ctx', 'tp')), may hold values from -0.09375 to 0.09375
- w_up: bfloat16 [32, 4096, 384], P(('ctx', 'tp')), may hold values from -0.09375 to 0.09375
- w_down: bfloat16 [32, 384, 4096], P(('ctx', 'tp')), may hold values from -0.21875 to 0.21875
- grad_out: bfloat16 [8192, 4096], P(('ctx', 'tp')), may hold values from -6 to 6
Outputs:
- d_ctx_heads: bfloat16 [8192, 4096], P('ctx', 'tp')
- d_out_weight: bfloat16 [4096, 4096], P('ctx', 'tp')
- d_hidden_in: bfloat16 [8192, 4096], P(('ctx', 'tp'))
- d_route_weights: float32 [8192, 2], P(('ctx', 'tp'))
- d_w_gate: bfloat16 [32, 4096, 384], P(('ctx', 'tp'))
- d_w_up: bfloat16 [32, 4096, 384], P(('ctx', 'tp'))
- d_w_down: bfloat16 [32, 384, 4096], P(('ctx', 'tp'))
Inputs may be any that keep to these rules, and one draw needn't show every extreme that they name: `expert_ids`: each token names 2 different experts. In each aligned block of 256 tokens (the tokens of one device) no expert is named by more than 48 tokens, a bound that some block reaches. Every expert is named by some token.
All inputs are finite; a program needn't handle non-finite values.
Results may differ from a plain program's by a relative error of at most 0.02.
Values may be sent and summed in bfloat16 or wider, within the bound.
No kernel may reach another device: no remote copies, remote signals or barrier semaphores. Data moves between devices by JAX's collectives and lax.ppermute only.
A program may use at most 192 MiB of HBM per device.

v0:
```python
import jax
import jax.numpy as jnp
from jax import lax
from jax.sharding import PartitionSpec as P

EPSILON = 1e-06
CONTRACT_FIRST = (((0,), (0,)), ((), ()))
CONTRACT_LAST = (((1,), (1,)), ((), ()))


def normalize(hidden_in, norm_gain):
    hidden_wide = hidden_in.astype(jnp.float32)
    rms_scale = lax.rsqrt(jnp.mean(hidden_wide * hidden_wide, axis=-1, keepdims=True) + EPSILON)
    normed = (hidden_wide * rms_scale * norm_gain).astype(jnp.bfloat16)
    return (hidden_wide, rms_scale, normed)


def norm_backward(hidden_wide, rms_scale, norm_gain, normed_grad, grad_out):
    gained = normed_grad * norm_gain
    inner = jnp.mean(gained * hidden_wide, axis=-1, keepdims=True)
    cubed = rms_scale * rms_scale * rms_scale
    return grad_out.astype(jnp.float32) + rms_scale * gained - hidden_wide * cubed * inner


def expert_half(slot_rows, slot_cots, slot_weights, gate_matrix, up_matrix, down_matrix):
    gate_pre = jnp.dot(slot_rows, gate_matrix, preferred_element_type=jnp.float32)
    up_value = jnp.dot(slot_rows, up_matrix, preferred_element_type=jnp.float32)
    sigmoid_gate = jax.nn.sigmoid(gate_pre)
    silu_gate = gate_pre * sigmoid_gate
    activated = (silu_gate * up_value).astype(jnp.bfloat16)
    back_proj = lax.dot_general(
        slot_cots, down_matrix, CONTRACT_LAST, preferred_element_type=jnp.float32
    )
    weight_dots = jnp.sum(activated.astype(jnp.float32) * back_proj, axis=-1)
    scaled_grad = (slot_weights[:, None] * slot_cots.astype(jnp.float32)).astype(jnp.bfloat16)
    down_wgrad = lax.dot_general(
        activated, scaled_grad, CONTRACT_FIRST, preferred_element_type=jnp.float32
    )
    act_grad = slot_weights[:, None] * back_proj
    gate_grad = (
        act_grad * up_value * sigmoid_gate * (1.0 + gate_pre * (1.0 - sigmoid_gate))
    ).astype(jnp.bfloat16)
    up_grad = (act_grad * silu_gate).astype(jnp.bfloat16)
    gate_wgrad = lax.dot_general(
        slot_rows, gate_grad, CONTRACT_FIRST, preferred_element_type=jnp.float32
    )
    up_wgrad = lax.dot_general(
        slot_rows, up_grad, CONTRACT_FIRST, preferred_element_type=jnp.float32
    )
    slot_grads = lax.dot_general(
        gate_grad, gate_matrix, CONTRACT_LAST, preferred_element_type=jnp.float32
    )
    slot_grads = slot_grads + lax.dot_general(
        up_grad, up_matrix, CONTRACT_LAST, preferred_element_type=jnp.float32
    )
    return (
        slot_grads.astype(jnp.bfloat16),
        weight_dots,
        gate_wgrad.astype(jnp.bfloat16),
        up_wgrad.astype(jnp.bfloat16),
        down_wgrad.astype(jnp.bfloat16),
    )


def per_device(
    ctx_heads,
    out_weight,
    hidden_in,
    norm_gain,
    expert_ids,
    route_weights,
    w_gate,
    w_up,
    w_down,
    grad_out,
):
    tok_rows, features = hidden_in.shape
    pick_count = expert_ids.shape[1]
    devices = lax.axis_size(("ctx", "tp"))
    experts = devices // 2
    capacity = 3 * tok_rows * pick_count // (2 * experts)
    hidden_wide, rms_scale, normed = normalize(hidden_in, norm_gain)
    flat_ids = expert_ids.reshape(-1)
    onehot = (flat_ids[:, None] == jnp.arange(experts, dtype=jnp.int32)[None, :]).astype(jnp.int32)
    slot_rank = jnp.sum((jnp.cumsum(onehot, axis=0) - onehot) * onehot, axis=1)
    target = flat_ids * capacity + slot_rank
    source = jnp.arange(tok_rows * pick_count, dtype=jnp.int32) // pick_count
    send_rows = (
        jnp.zeros((experts * capacity, features), jnp.bfloat16).at[target].set(normed[source])
    )
    send_grads = (
        jnp.zeros((experts * capacity, features), jnp.bfloat16).at[target].set(grad_out[source])
    )
    send_weights = (
        jnp.zeros((experts * capacity,), jnp.float32).at[target].set(route_weights.reshape(-1))
    )
    gate_matrix = w_gate[0]
    up_matrix = w_up[0]
    down_matrix = w_down[0]
    twice_rows = jnp.repeat(send_rows.reshape(experts, capacity, features), 2, axis=0)
    twice_grads = jnp.repeat(send_grads.reshape(experts, capacity, features), 2, axis=0)
    twice_weights = jnp.repeat(send_weights.reshape(experts, capacity), 2, axis=0)
    recv_rows, recv_grads, recv_weights = (
        lax.all_to_all(twice_rows, ("ctx", "tp"), split_axis=0, concat_axis=0, tiled=True),
        lax.all_to_all(twice_grads, ("ctx", "tp"), split_axis=0, concat_axis=0, tiled=True),
        lax.all_to_all(
            twice_weights.astype(jnp.bfloat16),
            ("ctx", "tp"),
            split_axis=0,
            concat_axis=0,
            tiled=True,
        ).astype(twice_weights.dtype),
    )
    slot_grads, weight_dots, gate_wgrad, up_wgrad, down_wgrad = expert_half(
        recv_rows.reshape(-1, features),
        recv_grads.reshape(-1, features),
        recv_weights.reshape(-1),
        gate_matrix,
        up_matrix,
        down_matrix,
    )
    back_rows, back_dots = (
        lax.all_to_all(
            slot_grads.reshape(devices, capacity, features),
            ("ctx", "tp"),
            split_axis=0,
            concat_axis=0,
            tiled=True,
        ),
        lax.all_to_all(
            weight_dots.reshape(devices, capacity).astype(jnp.bfloat16),
            ("ctx", "tp"),
            split_axis=0,
            concat_axis=0,
            tiled=True,
        ).astype(jnp.float32),
    )
    summed_rows = (
        back_rows.reshape(experts, 2, capacity, features)
        .astype(jnp.float32)
        .sum(axis=1)
        .astype(jnp.bfloat16)
    )
    summed_dots = back_dots.reshape(experts, 2, capacity).sum(axis=1)
    picked_rows = summed_rows.reshape(experts * capacity, features)[target]
    normed_grad = (
        picked_rows.reshape(tok_rows, pick_count, features).astype(jnp.float32).sum(axis=1)
    )
    route_grads = summed_dots.reshape(-1)[target].reshape(tok_rows, pick_count)
    resid_grad = norm_backward(hidden_wide, rms_scale, norm_gain, normed_grad, grad_out).astype(
        jnp.bfloat16
    )
    grads_all = lax.all_gather(resid_grad, "tp", axis=0, tiled=True)
    columns = grads_all
    heads_grad = jnp.dot(
        columns,
        lax.all_gather(out_weight, "ctx", axis=0, tiled=True),
        preferred_element_type=jnp.float32,
    ).astype(jnp.bfloat16)
    columns = grads_all
    weight_grad = lax.psum_scatter(
        lax.dot_general(
            columns, ctx_heads, CONTRACT_FIRST, preferred_element_type=jnp.float32
        ).astype(jnp.bfloat16),
        "ctx",
        scatter_dimension=0,
        tiled=True,
    )
    return (
        heads_grad,
        weight_grad,
        resid_grad,
        route_grads,
        gate_wgrad[None],
        up_wgrad[None],
        down_wgrad[None],
    )


def solution(mesh):
    in_specs = (
        P("ctx", "tp"),
        P("ctx", "tp"),
        P(("ctx", "tp"), None),
        P(),
        P(("ctx", "tp"), None),
        P(("ctx", "tp"), None),
        P(("ctx", "tp"), None, None),
        P(("ctx", "tp"), None, None),
        P(("ctx", "tp"), None, None),
        P(("ctx", "tp"), None),
    )
    out_specs = (
        P("ctx", "tp"),
        P("ctx", "tp"),
        P(("ctx", "tp"), None),
        P(("ctx", "tp"), None),
        P(("ctx", "tp"), None, None),
        P(("ctx", "tp"), None, None),
        P(("ctx", "tp"), None, None),
    )
    return jax.shard_map(
        per_device, mesh=mesh, in_specs=in_specs, out_specs=out_specs, check_vma=False
    )
```

profile of v0, /device:TPU:0, one launch (start us, length us, event | category | flops | bytes accessed | tf_op | source)
XLA Modules:
  0.0 1298.9 jit_solution(8146687305813518773)
XLA Ops:
  7.2 0.0 copy-start
  7.2 0.8 broadcast_multiply_fusion
  8.0 0.9 copy.31
  9.0 0.1 eq.29
  9.1 0.1 eq.25
  9.2 0.1 copy.30
  9.4 0.1 mul.129
  9.5 1.2 reduce-window.6
  10.7 0.2 slice_reduce_fusion
  11.0 0.8 copy.34
  11.8 0.1 reshape.254
  11.9 0.1 fusion.31
  12.0 2.4 scatter_custom_fusion
  14.5 0.1 convert_element_type.119
  14.6 0.6 copy.35
  15.2 7.8 all-to-all-start
  23.1 2.1 fusion.6
  25.2 3.5 fusion.8
  28.7 19.6 %scatter_custom_fusion.2 = bf16[768,4096]{1,0:T(8,128)(2,1)} fusion(s32[512]{0:T(512)S(1)} %bitcast.81, bf16[256,4096]{1,0:T(8,128)(2,1)} %fusion.8, s32[1024]{0:T(1024)S(1)} %pad_clamp_fusion.1, bf16[]{:T(256)} %constant.37.clone.1), kind=kCustom, calls=%fused_computation.30 | custom fusion | bytes 6291968 | tf_op jit(solution)/shard_map/scatter | solution.py:89
  48.3 0.0 all-to-all-done
  48.3 8.4 broadcast_in_dim.17
  56.8 6.3 all-to-all-start.2
  63.0 19.7 %scatter_custom_fusion.1 = bf16[768,4096]{1,0:T(8,128)(2,1)} fusion(s32[512]{0:T(512)S(1)} %bitcast.82, bf16[256,4096]{1,0:T(8,128)(2,1)} %param.19, s32[1024]{0:T(1024)S(1)} %pad_clamp_fusion.1, bf16[]{:T(256)} %constant.37.clone.1), kind=kCustom, calls=%fused_computation.32 | custom fusion | bytes 6291968 | tf_op jit(solution)/shard_map/scatter | solution.py:92
  82.8 251.2 %all-to-all-done.2 = bf16[32,48,4096]{2,1,0:T(8,128)(2,1)} async-done(((bf16[32,48,4096]{2,1,0:T(8,128)(2,1)}), bf16[32,48,4096]{2,1,0:T(8,128)(2,1)}, u32[]{:S(2)}, u32[]{:S(2)}) %all-to-all-start.2) | async-done | bytes 12582944 | tf_op jit(solution)/shard_map/all_to_all | solution.py:104
  333.9 8.4 broadcast_in_dim.16
  342.4 11.5 all-to-all-start.1
  353.9 0.1 convert_reduce_fusion
  354.0 0.1 reshape.215
  354.0 9.7 fusion.19
  363.7 9.6 fusion.22
  373.3 251.5 %all-to-all-done.1 = bf16[32,48,4096]{2,1,0:T(8,128)(2,1)} async-done(((bf16[32,48,4096]{2,1,0:T(8,128)(2,1)}), bf16[32,48,4096]{2,1,0:T(8,128)(2,1)}, u32[]{:S(2)}, u32[]{:S(2)}) %all-to-all-start.1) | async-done | bytes 12582944 | tf_op jit(solution)/shard_map/all_to_all | solution.py:105
  624.8 16.6 %multiply_reduce_fusion = (bf16[1536]{0:T(1024)(128)(2,1)S(1)}, bf16[1536,384]{0,1:T(8,128)(2,1)}, bf16[1536,384]{0,1:T(8,128)(2,1)S(1)}, bf16[1536,384]{0,1:T(8,128)(2,1)}) fusion(f32[1536,384]{0,1:T(8,128)} %fusion.22, f32[1536,384]{0,1:T(8,128)} %fusion.19, f32[1536]{0:T(1024)S(1)} %reshape.215, bf16[1536,4096]{1,0:T(8,128)(2,1)} %bitcast.7, ...), kind=kOutput, calls=%fused_computation.45 | convolution fusion | flops 4843043328 | bytes 23995392 | tf_op jit(solution)/shard_map/dot_general | solution.py:31
  641.4 11.8 fusion.17
  653.2 16.0 %add_convert_fusion = bf16[1536,4096]{1,0:T(8,128)(2,1)} fusion(f32[1536,4096]{1,0:T(8,128)} %fusion.17, bf16[1536,384]{0,1:T(8,128)(2,1)} %get-tuple-element.31, bf16[1,4096,384]{2,1,0:T(8,128)(2,1)} %param.17), kind=kOutput, calls=%fused_computation.8 | convolution fusion | flops 4844421120 | bytes 42074112 | tf_op jit(solution)/shard_map/dot_general | solution.py:53
  669.2 11.3 all-to-all-start.3
  680.6 0.0 all-gather.3.cloned.1.call-start
  680.6 270.9 %all-to-all-done.3 = bf16[32,48,4096]{2,1,0:T(8,128)(2,1)} async-done(((bf16[32,48,4096]{2,1,0:T(8,128)(2,1)}), bf16[32,48,4096]{2,1,0:T(8,128)(2,1)}, u32[]{:S(2)}, u32[]{:S(2)}) %all-to-all-start.3) | async-done | bytes 12582944 | tf_op jit(solution)/shard_map/all_to_all | solution.py:123
  951.5 11.3 bitcast_reduce_fusion
  962.8 12.2 gather_fusion
  974.9 9.6 reshape.216
  984.6 13.6 %reduce_sum.72 = f32[256,4096]{1,0:T(8,128)} reduce(f32[256,2,4096]{2,1,0:T(2,128)} %reshape.216, f32[]{:T(128)} %constant.31.clone.1), dimensions={1}, to_apply=%region_8.9 | reduce | flops 1048576 | bytes 12582916 | tf_op jit(solution)/shard_map/reduce_sum | solution.py:147
  998.2 3.0 fusion.12
  1001.2 0.5 copy-done.2
  1001.7 0.7 copy-done.5
  1002.3 3.3 fusion.11
  1005.6 0.0 all-gather.3.cloned.1.call-update
  1005.6 0.0 all-gather.5.cloned.1.call-start
  1005.7 0.7 all-gather.5.cloned.1.call-update
  1006.4 0.0 reduce-scatter.2.cloned.1.call-start
  1006.4 155.6 %all-gather.3.cloned.1.call-done = bf16[1024,4096]{1,0:T(8,128)(2,1)} async-done(((bf16[256,4096]{1,0:T(8,128)(2,1)}), bf16[1024,4096]{1,0:T(8,128)(2,1)}) %all-gather.3.cloned.1.call-update) | async-done | bytes 8388624 | tf_op jit(solution)/shard_map/all_gather | solution.py:153
  1162.1 15.1 %convolution_convert_fusion = bf16[4096,1024]{1,0:T(8,128)(2,1)} fusion(bf16[1024,4096]{1,0:T(8,128)(2,1)} %all-gather.3.cloned.1.call-done, bf16[1024,1024]{1,0:T(8,128)(2,1)} %param.10), kind=kOutput, calls=%fused_computation.12 | convolution fusion | flops 8594128896 | bytes 18874368 | tf_op jit(solution)/shard_map/dot_general | solution.py:162
  1177.2 0.0 reduce-scatter.2.cloned.1.call-update
  1177.2 0.7 convert_element_type.146
  1177.9 2.8 all-to-all-start.4
  1180.7 11.0 fusion.3
  1191.7 11.0 fusion.4
  1202.8 11.3 fusion.5
  1214.1 0.0 all-to-all-done.4
  1214.2 0.1 reshape.213
  1214.2 2.3 gather_fusion.1
  1216.5 0.1 reshape.214
  1216.7 0.7 copy.37
  1217.3 15.0 %convolution_convert_fusion.3 = bf16[1024,1024]{1,0:T(8,128)(2,1)} fusion(bf16[1024,4096]{1,0:T(8,128)(2,1)} %all-gather.3.cloned.1.call-done, bf16[4096,1024]{1,0:T(8,128)(2,1)} %all-gather.5.cloned.1.call-done), kind=kOutput, calls=%fused_computation.51 | convolution fusion | flops 8590983168 | bytes 18874368 | tf_op jit(solution)/shard_map/dot_general | solution.py:155
  1232.3 59.8 %reduce-scatter.2.cloned.1.call-done = bf16[512,1024]{1,0:T(8,128)(2,1)} async-done(((bf16[4096,1024]{1,0:T(8,128)(2,1)}), bf16[512,1024]{1,0:T(8,128)(2,1)}) %reduce-scatter.2.cloned.1.call-update) | async-done | bytes 1048592 | tf_op jit(solution)/shard_map/reduce_scatter | solution.py:161
  (33 shorter events, 0.2 us)
Async XLA Ops:
  7.2 346.9 %copy-start = (bf16[1,4096,384]{2,1,0:T(8,128)(2,1)S(1)}, bf16[1,4096,384]{2,1,0:T(8,128)(2,1)}, u32[]{:S(2)}) copy-start(bf16[1,4096,384]{2,1,0:T(8,128)(2,1)} %param.16) | copy-start | bytes 9437188
  15.2 33.1 %all-to-all-start = ((bf16[32,1,48]{2,1,0:T(2,128)(2,1)}), bf16[32,1,48]{2,1,0:T(2,128)(2,1)S(1)}, u32[]{:S(2)}, u32[]{:S(2)}) async-start(bf16[32,1,48]{2,1,0:T(2,128)(2,1)} %copy.35), calls=%async_computation | async-start | bytes 32768 | tf_op jit(solution)/shard_map/all_to_all | solution.py:106
  56.8 277.2 %all-to-all-start.2 = ((bf16[32,48,4096]{2,1,0:T(8,128)(2,1)}), bf16[32,48,4096]{2,1,0:T(8,128)(2,1)}, u32[]{:S(2)}, u32[]{:S(2)}) async-start(bf16[32,48,4096]{2,1,0:T(8,128)(2,1)} %bitcast.75), calls=%async_computation.2 | async-start | bytes 25165824 | tf_op jit(solution)/shard_map/all_to_all | solution.py:104
  342.4 282.4 %all-to-all-start.1 = ((bf16[32,48,4096]{2,1,0:T(8,128)(2,1)}), bf16[32,48,4096]{2,1,0:T(8,128)(2,1)}, u32[]{:S(2)}, u32[]{:S(2)}) async-start(bf16[32,48,4096]{2,1,0:T(8,128)(2,1)} %bitcast.74), calls=%async_computation.1 | async-start | bytes 25165824 | tf_op jit(solution)/shard_map/all_to_all | solution.py:105
  354.0 9.7 copy-start.4
  641.4 11.8 copy-start.7
  669.2 282.3 %all-to-all-start.3 = ((bf16[32,48,4096]{2,1,0:T(8,128)(2,1)}), bf16[32,48,4096]{2,1,0:T(8,128)(2,1)}, u32[]{:S(2)}, u32[]{:S(2)}) async-start(bf16[32,48,4096]{2,1,0:T(8,128)(2,1)} %bitcast.73), calls=%async_computation.3 | async-start | bytes 25165824 | tf_op jit(solution)/shard_map/all_to_all | solution.py:123
  680.6 481.5 %all-gather.3.cloned.1.call-start = ((), (), s32[]{:S(2)}) async-start(), calls=%async_computation.6 | async-start | bytes 10485760 | tf_op jit(solution)/shard_map/all_gather | solution.py:153
  984.6 13.6 %copy-start.3 = (bf16[256,4096]{1,0:T(8,128)(2,1)S(1)}, bf16[256,4096]{1,0:T(8,128)(2,1)}, u32[]{:S(2)}) copy-start(bf16[256,4096]{1,0:T(8,128)(2,1)} %param.12) | copy-start | bytes 6291460
  984.6 13.6 %copy-start.9 = (f32[4096]{0:T(1024)S(1)}, f32[4096]{0:T(1024)}, u32[]{:S(2)}) copy-start(f32[4096]{0:T(1024)} %param.13) | copy-start | bytes 49156
  998.2 3.5 copy-start.2
  998.2 4.1 copy-start.5
  1005.6 211.7 %all-gather.5.cloned.1.call-start = ((), (), s32[]{:S(2)}) async-start(), calls=%async_computation.7 | async-start | bytes 9437184 | tf_op jit(solution)/shard_map/all_gather | solution.py:157
  1006.4 285.7 %reduce-scatter.2.cloned.1.call-start = ((), (), s32[]{:S(2)}) async-start(), calls=%async_computation.8 | async-start | bytes 9437184 | tf_op jit(solution)/shard_map/reduce_scatter | solution.py:161
  1177.2 3.5 copy-start.8
  1177.9 36.2 %all-to-all-start.4 = ((bf16[32,1,48]{2,1,0:T(2,128)(2,1)}), bf16[32,1,48]{2,1,0:T(2,128)(2,1)S(1)}, u32[]{:S(2)}, u32[]{:S(2)}) async-start(bf16[32,1,48]{2,1,0:T(2,128)(2,1)} %convert_element_type.146), calls=%async_computation.5 | async-start | bytes 32768 | tf_op jit(solution)/shard_map/all_to_all | solution.py:130
  1180.7 11.0 copy-start.6
  1191.7 11.0 copy-start.10
  1217.3 74.8 %copy-start.1 = (bf16[1,4096,384]{2,1,0:T(8,128)(2,1)S(1)}, bf16[1,4096,384]{2,1,0:T(8,128)(2,1)}, u32[]{:S(2)}) copy-start(bf16[1,4096,384]{2,1,0:T(8,128)(2,1)} %param.16) | copy-start | bytes 9437188
Sparse Core Ops, SparseCore 0:
  1005.7 156.2 all-gather.2
  1163.9 52.7 all-gather.4
  1220.8 71.2 reduce-scatter.1
where the time goes:
time: 1300 us
  waiting for transfers between devices  990 us (76%)
  matrix products  127 us (10%)
  local copies, waits for them, and re-layouts  89 us (7%)
  starting transfers between devices  39.9 us (3%)
  other arithmetic  39 us (3%)
  between operations  14.2 us (1%)
    all_to_all x1, waiting for transfers between devices, per_device(): lax.all_to_all(slot_grads.reshape(devices, capacity, features), ('ctx', '...  271 us
    all_to_all x1, waiting for transfers between devices, per_device(): lax.all_to_all(twice_grads, ('ctx', 'tp'), split_axis=0, concat_axis=0, t...  251 us
    all_to_all x1, waiting for transfers between devices, per_device(): lax.all_to_all(twice_rows, ('ctx', 'tp'), split_axis=0, concat_axis=0, ti...  251 us
    all_gather x1, waiting for transfers between devices, per_device(): grads_all = lax.all_gather(resid_grad, 'tp', axis=0, tiled=True)  156 us
    reduce_scatter x1, waiting for transfers between devices, per_device(): lax.psum_scatter(lax.dot_general(columns, ctx_heads, CONTRACT_FIRST, pref...  59.8 us
    scatter x2, local copies, waits for them, and re-layouts, per_device(): jnp.zeros((experts * capacity, features), jnp.bfloat16).at[target]  39.3 us
  transfers between devices with their start and end apart: 8, of which 5 were waited for; matrix products, arithmetic and copies ran while one was open for 10% of the time, Pallas kernels for 0%

commit v1 on v0

--- a/solution.py
+++ b/solution.py
@@ -59,6 +59,250 @@
         gate_wgrad.astype(jnp.bfloat16),
         up_wgrad.astype(jnp.bfloat16),
         down_wgrad.astype(jnp.bfloat16),
+    )
+
+
+END_TO_MID = ((0, 1), (3, 2))
+MID_TO_MID = ((1, 2), (2, 1))
+MID_TO_END = ((1, 0), (2, 3))
+ARRIVAL = ((0, 1, 2, 3), (1, 2, 0, 3), (2, 1, 3, 0), (3, 2, 1, 0))
+TOKEN_CHUNKS = 4
+ROUTING_COLUMNS = 128
+
+
+def hop(array, pairs):
+    return lax.ppermute(array, "tp", pairs)
+
+
+def after(array, *earlier):
+    return lax.optimization_barrier((array,) + earlier)[0]
+
+
+def slot_choice(ids, expert_list, capacity):
+    hits = jnp.any(ids[..., None, :, :] == expert_list[:, None, None], axis=-2)
+    tokens = ids.shape[-1]
+    before = jnp.triu(jnp.ones((tokens, tokens), jnp.bfloat16), 1)
+    ranks = jnp.dot(hits.astype(jnp.bfloat16), before, preferred_element_type=jnp.float32)
+    slots = jnp.arange(capacity, dtype=jnp.float32)
+    return hits[..., None, :] & (ranks[..., None, :] == slots[:, None])
+
+
+def expert_block(rows, cots, weights, gate_matrix, up_matrix, down_matrix):
+    gate_pre = jnp.dot(rows, gate_matrix, preferred_element_type=jnp.float32)
+    up_value = jnp.dot(rows, up_matrix, preferred_element_type=jnp.float32)
+    back_proj = lax.dot_general(cots, down_matrix, CONTRACT_LAST, preferred_element_type=jnp.float32)
+    sigmoid_gate = jax.nn.sigmoid(gate_pre)
+    silu_gate = gate_pre * sigmoid_gate
+    activated = silu_gate * up_value
+    weight_dots = jnp.sum(activated * back_proj, axis=-1)
+    weighted = (weights[:, None] * activated).astype(jnp.bfloat16)
+    act_grad = weights[:, None] * back_proj
+    gate_grad = (
+        act_grad * up_value * sigmoid_gate * (1.0 + gate_pre * (1.0 - sigmoid_gate))
+    ).astype(jnp.bfloat16)
+    up_grad = (act_grad * silu_gate).astype(jnp.bfloat16)
+    slot_grads = lax.dot_general(
+        gate_grad, gate_matrix, CONTRACT_LAST, preferred_element_type=jnp.float32
+    ) + lax.dot_general(up_grad, up_matrix, CONTRACT_LAST, preferred_element_type=jnp.float32)
+    return (slot_grads.astype(jnp.bfloat16), weight_dots, weighted, gate_grad, up_grad)
+
+
+def wide_sum(*terms):
+    total = terms[0].astype(jnp.float32)
+    for term in terms[1:]:
+        total = total + term.astype(jnp.float32)
+    return total
+
+
+def exchange(array):
+    return lax.all_to_all(array, "ctx", split_axis=0, concat_axis=0, tiled=True)
+
+
+def per_device_line(
+    ctx_heads,
+    out_weight,
+    hidden_in,
+    norm_gain,
+    expert_ids,
+    route_weights,
+    w_gate,
+    w_up,
+    w_down,
+    grad_out,
+):
+    tok_rows, features = hidden_in.shape
+    pick_count = expert_ids.shape[1]
+    n_ctx, n_tp = lax.axis_size("ctx"), lax.axis_size("tp")
+    experts = n_ctx * n_tp // 2
+    capacity = 3 * tok_rows * pick_count // (2 * experts)
+    ctx_at, tp_at = lax.axis_index("ctx"), lax.axis_index("tp")
+    arrival = jnp.array(ARRIVAL, jnp.int32)[tp_at]
+    gate_matrix, up_matrix, down_matrix = w_gate[0], w_up[0], w_down[0]
+
+    hidden_wide, rms_scale, normed = normalize(hidden_in, norm_gain)
+    plane_experts = (jnp.arange(n_ctx) * (n_tp // 2) + tp_at // 2).astype(jnp.float32)
+    own_expert = (ctx_at * (n_tp // 2) + tp_at // 2).astype(jnp.float32)
+
+    id_at, weight_at = 2 * features, 2 * features + pick_count
+    spare = ROUTING_COLUMNS - 2 * pick_count
+    own_block = jnp.concatenate(
+        [
+            grad_out,
+            normed,
+            expert_ids.astype(jnp.bfloat16),
+            route_weights.astype(jnp.bfloat16),
+            jnp.zeros((tok_rows, spare), jnp.bfloat16),
+        ],
+        axis=1,
+    )
+
+    def choose(block):
+        ids = block[:, id_at:weight_at].astype(jnp.float32).T
+        choice = slot_choice(ids, plane_experts, capacity).astype(jnp.bfloat16)
+        return choice.reshape(n_ctx * capacity, tok_rows)
+
+    def pack(choice, block):
+        packed = jnp.dot(choice, block, preferred_element_type=jnp.float32)
+        return packed.astype(jnp.bfloat16).reshape(n_ctx, capacity, -1)
+
+    def experts_on(slots):
+        slots = slots.reshape(n_ctx * capacity, -1)
+        cots, rows = slots[:, :features], slots[:, features:id_at]
+        named = slots[:, id_at:weight_at].astype(jnp.float32) == own_expert
+        pick_weights = slots[:, weight_at : weight_at + pick_count].astype(jnp.float32)
+        weights = jnp.sum(jnp.where(named, pick_weights, 0.0), axis=1)
+        slot_grads, weight_dots, weighted, gate_grad, up_grad = expert_block(
+            rows, cots, weights, gate_matrix, up_matrix, down_matrix
+        )
+        return (
+            slot_grads.reshape(n_ctx, capacity, features),
+            weight_dots.reshape(n_ctx, capacity),
+            (slots, weighted, gate_grad, up_grad),
+        )
+
+    def combine(choice, returned):
+        return lax.dot_general(
+            choice,
+            returned.reshape(n_ctx * capacity, features),
+            CONTRACT_FIRST,
+            preferred_element_type=jnp.float32,
+        ).astype(jnp.bfloat16)
+
+    from_end = hop(own_block, END_TO_MID)
+    from_mid = hop(own_block, MID_TO_MID)
+    near_mid = hop(own_block, MID_TO_END)
+    choice0 = choose(own_block)
+    slots0 = exchange(pack(choice0, own_block))
+    grads0, dots0, kept0 = experts_on(slots0)
+    back0 = exchange(grads0)
+    far_end = hop(after(from_end, grads0), MID_TO_MID)
+    far_mid = hop(after(from_mid, grads0), MID_TO_END)
+    block1 = from_mid + near_mid
+    choice1 = choose(block1)
+    slots1 = exchange(after(pack(choice1, block1), back0))
+    part0 = combine(choice0, back0)
+    last = hop(after(far_end, slots1), MID_TO_END)
+    block2 = from_end + far_mid
+    choice2 = choose(block2)
+    slots2 = exchange(after(pack(choice2, block2), slots1))
+    grads1, dots1, kept1 = experts_on(slots1)
+    back1 = exchange(after(grads1, slots2))
+    grads2, dots2, kept2 = experts_on(slots2)
+    back2 = exchange(after(grads2, back1))
+    block3 = far_end + last
+    choice3 = choose(block3)
+    part1 = combine(choice1, back1)
+    slots3 = exchange(after(pack(choice3, block3), back2))
+    part2 = combine(choice2, back2)
+    grads3, dots3, kept3 = experts_on(slots3)
+    back3 = exchange(grads3)
+    part3 = combine(choice3, back3)
+
+    def residual(total, at):
+        return norm_backward(
+            hidden_wide[at], rms_scale[at], norm_gain, total, grad_out[at]
+        ).astype(jnp.bfloat16)
+
+    whole = slice(0, tok_rows)
+    halves = [slice(i * tok_rows // 2, (i + 1) * tok_rows // 2) for i in range(2)]
+    from_near = hop(part1, END_TO_MID)
+    from_far = []
+    for at in halves:
+        to_far = wide_sum(hop(part2[at], END_TO_MID), part1[at]).astype(jnp.bfloat16)
+        from_far.append(hop(to_far, MID_TO_MID))
+    mid_sum = wide_sum(part0, from_near, jnp.concatenate(from_far, axis=0))
+    mid_resid = residual(mid_sum, whole)
+    far_mid = hop(mid_resid, MID_TO_MID)
+    near_mid = hop(mid_resid, MID_TO_END)
+    last_mid = hop(far_mid, MID_TO_END)
+    step = tok_rows // TOKEN_CHUNKS
+    own, second, third = [], [], []
+    for chunk in range(TOKEN_CHUNKS):
+        at = slice(chunk * step, (chunk + 1) * step)
+        passing = wide_sum(hop(part3[at], END_TO_MID), part3[at]).astype(jnp.bfloat16)
+        passing = wide_sum(hop(passing, MID_TO_MID), part2[at]).astype(jnp.bfloat16)
+        total = wide_sum(mid_sum[at], hop(passing, MID_TO_END))
+        resid = residual(total, at)
+        near_end = hop(resid, END_TO_MID)
+        far_end = hop(near_end, MID_TO_MID)
+        last_end = hop(far_end, MID_TO_END)
+        own.append(resid)
+        second.append(last_mid[at] + near_end)
+        third.append(far_end + last_end)
+    resid_grad = jnp.concatenate(own, axis=0)
+    columns = jnp.concatenate(own + [far_mid + near_mid] + second + third, axis=0)
+
+    heads = ctx_heads.shape[1]
+    head_rows = ctx_heads.reshape(n_tp, tok_rows, heads)[arrival].reshape(n_tp * tok_rows, heads)
+    weight_term = lax.dot_general(
+        columns, head_rows, CONTRACT_FIRST, preferred_element_type=jnp.float32
+    ).astype(jnp.bfloat16)
+    weight_grad = lax.psum_scatter(weight_term, "ctx", scatter_dimension=0, tiled=True)
+    projection = lax.all_gather(after(out_weight, back3), "ctx", axis=0, tiled=True)
+    heads_total = jnp.dot(
+        after(columns, weight_term), projection, preferred_element_type=jnp.float32
+    )
+    place_of = jnp.argsort(arrival)
+    heads_grad = (
+        heads_total.astype(jnp.bfloat16)
+        .reshape(n_tp, tok_rows, heads)[place_of]
+        .reshape(n_tp * tok_rows, heads)
+    )
+
+    def weight_grads(kept):
+        slots, weighted, gate_grad, up_grad = kept
+        cots, rows = slots[:, :features], slots[:, features:id_at]
+        return [
+            lax.dot_general(left, right, CONTRACT_FIRST, preferred_element_type=jnp.float32)
+            for left, right in ((weighted, cots), (rows, gate_grad), (rows, up_grad))
+        ]
+
+    early = [jnp.concatenate(parts, axis=0) for parts in zip(kept0, kept1, kept2)]
+    early = weight_grads([after(array, back2) for array in early])
+    late = weight_grads([after(array, weight_term) for array in kept3])
+    down_wgrad, gate_wgrad, up_wgrad = (
+        (first + then).astype(jnp.bfloat16) for first, then in zip(early, late)
+    )
+
+    block_dots = jnp.stack([dots0, dots1, dots2, dots3], axis=0)[place_of]
+    sent_dots = block_dots.transpose(1, 0, 2).reshape(n_ctx * n_tp, capacity)
+    own_dots = lax.all_to_all(
+        after(sent_dots, back3), ("ctx", "tp"), split_axis=0, concat_axis=0, tiled=True
+    )
+    own_dots = own_dots.reshape(experts, 2, capacity).sum(axis=1)
+    all_experts = jnp.arange(experts, dtype=jnp.float32)
+    own_choice = slot_choice(expert_ids.astype(jnp.float32).T, all_experts, capacity)
+    token_dots = jnp.sum(jnp.where(own_choice, own_dots[:, :, None], 0.0), axis=1)
+    named = expert_ids[:, :, None] == jnp.arange(experts, dtype=jnp.int32)
+    route_grads = jnp.sum(jnp.where(named, token_dots.T[:, None, :], 0.0), axis=-1)
+    return (
+        heads_grad,
+        weight_grad,
+        resid_grad,
+        route_grads,
+        gate_wgrad[None],
+        up_wgrad[None],
+        down_wgrad[None],
     )
 
 
@@ -199,6 +443,7 @@
         P(("ctx", "tp"), None, None),
         P(("ctx", "tp"), None, None),
     )
+    body = per_device_line if mesh.shape["tp"] == 4 else per_device
     return jax.shard_map(
-        per_device, mesh=mesh, in_specs=in_specs, out_specs=out_specs, check_vma=False
-    )
+        body, mesh=mesh, in_specs=in_specs, out_specs=out_specs, check_vma=False
+    )

time: 1300 us -> 1060 us (0.82)
  waiting for transfers between devices: 990 us -> 611 us
  starting transfers between devices: 39.9 us -> 127 us
  matrix products: 127 us -> 193 us
  local copies, waits for them, and re-layouts: 89 us -> 36.3 us
  other arithmetic: 39 us -> 70.2 us
    all_to_all x5 -> x9, waiting for transfers between devices: 773 us -> 287 us  [the longest x8 287 us: exchange(): return lax.all_to_all(array, 'ctx', split_axis=0, concat_axis=0, tiled=True)]
    ppermute x0 -> x38, waiting for transfers between devices: none -> 324 us  [hop(): return lax.ppermute(array, 'tp', pairs)]
    all_gather x2 -> x1, waiting for transfers between devices: 156 us -> 0.01 us  [per_device_line(): lax.all_gather(after(out_weight, back3), 'ctx', axis=0, tiled=True)]
    ppermute x0 -> x38, starting transfers between devices: none -> 86.1 us  [hop(): return lax.ppermute(array, 'tp', pairs)]
    dot_general x10 -> x41, matrix products: 127 us -> 193 us  [the longest x6 46.7 us: weight_grads(): lax.dot_general(left, right, CONTRACT_FIRST, preferred_element_type=jnp.f...]
    reduce_scatter x1, waiting for transfers between devices: 59.8 us -> 0.01 us  [per_device_line(): lax.psum_scatter(weight_term, 'ctx', scatter_dimension=0, tiled=True)]
    scatter x3 -> x0, local copies, waits for them, and re-layouts: 41.8 us -> none  [the longest x2 39.3 us: per_device(): jnp.zeros((experts * capacity, features), jnp.bfloat16).at[target]]
    reduce_sum x4 -> x7, other arithmetic: 25 us -> 5.52 us  [the longest x4 4.64 us: experts_on(): weights = jnp.sum(jnp.where(named, pick_weights, 0.0), axis=1)]
  transfers between devices with their start and end apart: 8 -> 49, of which waited for: 5 -> 24; matrix products, arithmetic and copies ran while one was open for 10% -> 24% of each run, Pallas kernels for 0% -> 0%
where the time goes in v1:
time: 1060 us; the launch traced here: 1050 us
  waiting for transfers between devices  611 us (58%)
  matrix products  193 us (18%)
  starting transfers between devices  127 us (12%)
  other arithmetic  70.2 us (7%)
  local copies, waits for them, and re-layouts  36.3 us (3%)
  between operations  15.9 us (2%)
    ppermute x38, waiting for transfers between devices, hop(): return lax.ppermute(array, 'tp', pairs)  324 us
    all_to_all x8, waiting for transfers between devices, exchange(): return lax.all_to_all(array, 'ctx', split_axis=0, concat_axis=0, tiled=True)  287 us
    ppermute x38, starting transfers between devices, hop(): return lax.ppermute(array, 'tp', pairs)  86.1 us
    dot_general x6, matrix products, weight_grads(): lax.dot_general(left, right, CONTRACT_FIRST, preferred_element_type=jnp.f...  46.7 us
    all_to_all x8, starting transfers between devices, exchange(): return lax.all_to_all(array, 'ctx', split_axis=0, concat_axis=0, tiled=True)  38.1 us
    dot_general x4, matrix products, pack(): packed = jnp.dot(choice, block, preferred_element_type=jnp.float32)  26.9 us
  transfers between devices with their start and end apart: 49, of which 24 were waited for; matrix products, arithmetic and copies ran while one was open for 24% of the time, Pallas kernels for 0%

profile of v1, /device:TPU:0, one launch (start us, length us, event | category | flops | bytes accessed | tf_op | source)
XLA Modules:
  0.0 1054.0 jit_solution(15977149324301430392)
XLA Ops:
  16.5 8.4 concatenate.24
  24.9 6.8 convolution_convert_fusion.3
  31.7 5.2 all-to-all-start
  39.6 7.5 collective-permute-start.2
  48.3 61.4 %all-to-all-done = bf16[8,48,8320]{2,1,0:T(8,128)(2,1)} async-done(((bf16[8,48,8320]{2,1,0:T(8,128)(2,1)}), bf16[8,48,8320]{2,1,0:T(8,128)(2,1)}, u32[]{:S(2)}, u32[]{:S(2)}) %all-to-all-start) | async-done | bytes 6389792 | tf_op jit(solution)/shard_map/all_to_all | solution.py:118
  110.9 4.6 fusion.48
  115.6 3.8 fusion.36
  119.4 5.2 multiply_reduce_fusion.9
  131.4 4.9 all-to-all-start.1
  136.4 7.7 collective-permute-done.1
  144.1 4.5 add.204
  152.3 81.9 %collective-permute-done.3 = bf16[256,8320]{1,0:T(8,128)(2,1)} collective-permute-done((bf16[256,8320]{1,0:T(8,128)(2,1)}, bf16[256,8320]{1,0:T(8,128)(2,1)}, u32[]{:S(2)}, u32[]{:S(2)}) %collective-permute-start.3) | collective-permute-done | bytes 4259872 | tf_op jit(solution)/shard_map/ppermute | solution.py:74
  234.2 4.5 add.208
  243.5 6.7 convolution_convert_fusion.2
  250.2 4.8 all-to-all-start.2
  257.6 6.7 convolution_convert_fusion.1
  264.3 63.3 %all-to-all-done.2 = bf16[8,48,8320]{2,1,0:T(8,128)(2,1)} async-done(((bf16[8,48,8320]{2,1,0:T(8,128)(2,1)}), bf16[8,48,8320]{2,1,0:T(8,128)(2,1)}, u32[]{:S(2)}, u32[]{:S(2)}) %all-to-all-start.2) | async-done | bytes 6389792 | tf_op jit(solution)/shard_map/all_to_all | solution.py:118
  327.6 4.8 all-to-all-start.3
  334.9 4.6 fusion.45
  339.5 3.8 fusion.32
  343.4 4.7 multiply_reduce_fusion.8
  353.6 51.5 %all-to-all-done.3 = bf16[8,48,8320]{2,1,0:T(8,128)(2,1)} async-done(((bf16[8,48,8320]{2,1,0:T(8,128)(2,1)}), bf16[8,48,8320]{2,1,0:T(8,128)(2,1)}, u32[]{:S(2)}, u32[]{:S(2)}) %all-to-all-start.3) | async-done | bytes 6389792 | tf_op jit(solution)/shard_map/all_to_all | solution.py:118
  405.1 4.6 all-to-all-start.4
  410.9 4.6 fusion.42
  419.3 4.7 multiply_reduce_fusion.7
  429.6 18.0 %all-to-all-done.4 = bf16[8,48,4096]{2,1,0:T(8,128)(2,1)} async-done(((bf16[8,48,4096]{2,1,0:T(8,128)(2,1)}), bf16[8,48,4096]{2,1,0:T(8,128)(2,1)}, u32[]{:S(2)}, u32[]{:S(2)}) %all-to-all-start.4) | async-done | bytes 3145760 | tf_op jit(solution)/shard_map/all_to_all | solution.py:118
  447.6 4.4 all-to-all-start.5
  452.1 4.5 add.216
  460.7 6.7 convolution_convert_fusion
  467.4 22.6 %all-to-all-done.5 = bf16[8,48,4096]{2,1,0:T(8,128)(2,1)} async-done(((bf16[8,48,4096]{2,1,0:T(8,128)(2,1)}), bf16[8,48,4096]{2,1,0:T(8,128)(2,1)}, u32[]{:S(2)}, u32[]{:S(2)}) %all-to-all-start.5) | async-done | bytes 3145760 | tf_op jit(solution)/shard_map/all_to_all | solution.py:118
  489.9 4.9 all-to-all-start.6
  494.9 4.5 fusion.11
  512.8 54.6 %all-to-all-done.6 = bf16[8,48,8320]{2,1,0:T(8,128)(2,1)} async-done(((bf16[8,48,8320]{2,1,0:T(8,128)(2,1)}), bf16[8,48,8320]{2,1,0:T(8,128)(2,1)}, u32[]{:S(2)}, u32[]{:S(2)}) %all-to-all-start.6) | async-done | bytes 6389792 | tf_op jit(solution)/shard_map/all_to_all | solution.py:118
  567.5 4.6 fusion.39
  572.1 3.8 fusion.24
  577.1 4.6 multiply_reduce_fusion.6
  587.3 4.5 all-to-all-start.7
  591.9 4.1 add_convert_fusion.8
  606.8 7.2 multiply_reduce_fusion
  614.1 15.6 %all-to-all-done.7 = bf16[8,48,4096]{2,1,0:T(8,128)(2,1)} async-done(((bf16[8,48,4096]{2,1,0:T(8,128)(2,1)}), bf16[8,48,4096]{2,1,0:T(8,128)(2,1)}, u32[]{:S(2)}, u32[]{:S(2)}) %all-to-all-start.7) | async-done | bytes 3145760 | tf_op jit(solution)/shard_map/all_to_all | solution.py:118
  633.3 27.1 %collective-permute-start.17 = (bf16[64,4096]{1,0:T(8,128)(2,1)S(1)}, bf16[64,4096]{1,0:T(8,128)(2,1)S(1)}, u32[]{:S(2)}, u32[]{:S(2)}) collective-permute-start(bf16[64,4096]{1,0:T(8,128)(2,1)S(1)} %get-tuple-element.69), channel_id=1, source_target_pairs={{0,1},{3,2},{4,5},{7,6},{8,9},{11,10},{12,13},{15,14},{16,17},{19,... | collective-permute-start | bytes 1572872 | tf_op jit(solution)/shard_map/ppermute | solution.py:74
  672.7 11.2 %collective-permute-done.11 = bf16[64,4096]{1,0:T(8,128)(2,1)S(1)} collective-permute-done((bf16[64,4096]{1,0:T(8,128)(2,1)S(1)}, bf16[64,4096]{1,0:T(8,128)(2,1)S(1)}, u32[]{:S(2)}, u32[]{:S(2)}) %collective-permute-start.11) | collective-permute-done | bytes 524320 | tf_op jit(solution)/shard_map/ppermute | solution.py:74
  683.9 11.2 %collective-permute-done.14 = bf16[64,4096]{1,0:T(8,128)(2,1)S(1)} collective-permute-done((bf16[64,4096]{1,0:T(8,128)(2,1)S(1)}, bf16[64,4096]{1,0:T(8,128)(2,1)S(1)}, u32[]{:S(2)}, u32[]{:S(2)}) %collective-permute-start.14) | collective-permute-done | bytes 524320 | tf_op jit(solution)/shard_map/ppermute | solution.py:74
  695.2 9.0 collective-permute-done.20
  716.9 59.6 %collective-permute-done.22 = bf16[64,4096]{1,0:T(8,128)(2,1)S(1)} collective-permute-done((bf16[64,4096]{1,0:T(8,128)(2,1)}, bf16[64,4096]{1,0:T(8,128)(2,1)S(1)}, u32[]{:S(2)}, u32[]{:S(2)}) %collective-permute-start.22) | collective-permute-done | bytes 524320 | tf_op jit(solution)/shard_map/ppermute | solution.py:74
  777.8 10.1 collective-permute-done.13
  787.9 11.2 %collective-permute-done.16 = bf16[64,4096]{1,0:T(8,128)(2,1)} collective-permute-done((bf16[64,4096]{1,0:T(8,128)(2,1)}, bf16[64,4096]{1,0:T(8,128)(2,1)}, u32[]{:S(2)}, u32[]{:S(2)}) %collective-permute-start.16) | collective-permute-done | bytes 524320 | tf_op jit(solution)/shard_map/ppermute | solution.py:74
  799.1 11.1 %collective-permute-done.19 = bf16[64,4096]{1,0:T(8,128)(2,1)S(1)} collective-permute-done((bf16[64,4096]{1,0:T(8,128)(2,1)}, bf16[64,4096]{1,0:T(8,128)(2,1)S(1)}, u32[]{:S(2)}, u32[]{:S(2)}) %collective-permute-start.19) | collective-permute-done | bytes 524320 | tf_op jit(solution)/shard_map/ppermute | solution.py:74
  810.2 4.9 multiply_reduce_fusion.2
  823.5 31.6 %collective-permute-done.24 = bf16[256,4096]{1,0:T(8,128)(2,1)S(1)} collective-permute-done((bf16[256,4096]{1,0:T(8,128)(2,1)}, bf16[256,4096]{1,0:T(8,128)(2,1)S(1)}, u32[]{:S(2)}, u32[]{:S(2)}) %collective-permute-start.24) | collective-permute-done | bytes 2097184 | tf_op jit(solution)/shard_map/ppermute | solution.py:74
  864.1 33.2 %collective-permute-done.25 = bf16[256,4096]{1,0:T(8,128)(2,1)S(1)} collective-permute-done((bf16[256,4096]{1,0:T(8,128)(2,1)}, bf16[256,4096]{1,0:T(8,128)(2,1)S(1)}, u32[]{:S(2)}, u32[]{:S(2)}) %collective-permute-start.25) | collective-permute-done | bytes 2097184 | tf_op jit(solution)/shard_map/ppermute | solution.py:74
  903.2 11.4 %collective-permute-done.31 = bf16[64,4096]{1,0:T(8,128)(2,1)S(1)} collective-permute-done((bf16[64,4096]{1,0:T(8,128)(2,1)S(1)}, bf16[64,4096]{1,0:T(8,128)(2,1)S(1)}, u32[]{:S(2)}, u32[]{:S(2)}) %collective-permute-start.31) | collective-permute-done | bytes 524320 | tf_op jit(solution)/shard_map/ppermute | solution.py:74
  914.7 11.1 %collective-permute-done.33 = bf16[64,4096]{1,0:T(8,128)(2,1)S(1)} collective-permute-done((bf16[64,4096]{1,0:T(8,128)(2,1)S(1)}, bf16[64,4096]{1,0:T(8,128)(2,1)S(1)}, u32[]{:S(2)}, u32[]{:S(2)}) %collective-permute-start.33) | collective-permute-done | bytes 524320 | tf_op jit(solution)/shard_map/ppermute | solution.py:74
  925.9 11.1 %collective-permute-done.35 = bf16[64,4096]{1,0:T(8,128)(2,1)S(1)} collective-permute-done((bf16[64,4096]{1,0:T(8,128)(2,1)S(1)}, bf16[64,4096]{1,0:T(8,128)(2,1)S(1)}, u32[]{:S(2)}, u32[]{:S(2)}) %collective-permute-start.35) | collective-permute-done | bytes 524320 | tf_op jit(solution)/shard_map/ppermute | solution.py:74
  937.2 7.3 collective-permute-done.37
  947.8 11.3 %convolution_convert_fusion.4 = bf16[4096,1024]{1,0:T(8,128)(2,1)} fusion(bf16[1024,4096]{1,0:T(8,128)(2,1)S(1)} %add_dynamic-update-slice_fusion.1, bf16[1024,1024]{1,0:T(8,128)(2,1)S(1)} %bitcast.202), kind=kOutput, calls=%fused_computation.14 | convolution fusion | flops 8594128896 | bytes 18874368 | tf_op jit(solution)/shard_map/dot_general | solution.py:257
  961.6 12.3 %pad_maximum_fusion = bf16[1152,8320]{1,0:T(8,128)(2,1)S(1)} fusion(bf16[384,8320]{1,0:T(8,128)(2,1)} %bitcast.21, bf16[384,8320]{1,0:T(8,128)(2,1)} %bitcast.14, bf16[384,8320]{1,0:T(8,128)(2,1)} %bitcast.4), kind=kLoop, calls=%fused_computation.3 | loop fusion | flops 57507840 | bytes 38338560 | tf_op jit(solution)/shard_map/concatenate | solution.py:280
  973.9 8.3 fusion.4
  982.8 7.3 fusion.2
  994.4 11.3 %fusion = f32[384,4096]{1,0:T(8,128)} fusion(bf16[1152,384]{1,0:T(8,128)(2,1)} %pad_maximum_fusion.4, bf16[1152,8320]{1,0:T(8,128)(2,1)} %copy-done.10), kind=kOutput, calls=%fused_computation.8 | convolution fusion | flops 3623878656 | bytes 16613376 | tf_op jit(solution)/shard_map/dot_general | solution.py:276
  1008.2 7.8 fusion.8
  1016.0 6.0 fusion.6
  1022.0 5.9 fusion.7
  1028.0 15.1 %convolution_convert_fusion.5 = bf16[1024,1024]{1,0:T(8,128)(2,1)} fusion(bf16[1024,4096]{1,0:T(8,128)(2,1)} %copy-done.50, bf16[4096,1024]{1,0:T(8,128)(2,1)} %all-gather.2.cloned.1.call-done), kind=kOutput, calls=%fused_computation.94 | convolution fusion | flops 8590983168 | bytes 18874368 | tf_op jit(solution)/shard_map/dot_general | solution.py:262
  (306 shorter events, 155.6 us)
Async XLA Ops:
  7.2 108.4 %copy-start = (bf16[1,4096,384]{2,1,0:T(8,128)(2,1)S(1)}, bf16[1,4096,384]{2,1,0:T(8,128)(2,1)}, u32[]{:S(2)}) copy-start(bf16[1,4096,384]{2,1,0:T(8,128)(2,1)} %param.17) | copy-start | bytes 9437188
  12.6 229.7 %copy-start.59 = (f32[8]{0:T(128)}, f32[8]{0:T(128)S(1)}, u32[]{:S(2)}) copy-start(f32[8]{0:T(128)S(1)} %add_convert_fusion.17) | copy-start | bytes 100
  31.7 78.1 %all-to-all-start = ((bf16[8,48,8320]{2,1,0:T(8,128)(2,1)}), bf16[8,48,8320]{2,1,0:T(8,128)(2,1)}, u32[]{:S(2)}, u32[]{:S(2)}) async-start(bf16[8,48,8320]{2,1,0:T(8,128)(2,1)} %bitcast.191), calls=%async_computation | async-start | bytes 12779520 | tf_op jit(solution)/shard_map/all_to_all | solution.py:118
  36.9 93.3 %collective-permute-start = (bf16[256,8320]{1,0:T(8,128)(2,1)}, bf16[256,8320]{1,0:T(8,128)(2,1)}, u32[]{:S(2)}, u32[]{:S(2)}) collective-permute-start(bf16[256,8320]{1,0:T(8,128)(2,1)} %concatenate.24), channel_id=1, source_target_pairs={{1,2},{2,1},{5,6},{6,5},{9,10},{10,9},{13,14},{14,13},{17,18},{18,... | collective-permute-start | bytes 12779528 | tf_op jit(solution)/shard_map/ppermute | solution.py:74
  39.6 112.7 %collective-permute-start.2 = (bf16[256,8320]{1,0:T(8,128)(2,1)}, bf16[256,8320]{1,0:T(8,128)(2,1)}, u32[]{:S(2)}, u32[]{:S(2)}) collective-permute-start(bf16[256,8320]{1,0:T(8,128)(2,1)} %concatenate.24), channel_id=1, source_target_pairs={{0,1},{3,2},{4,5},{7,6},{8,9},{11,10},{12,13},{15,14},{16,17},{19,... | collective-permute-start | bytes 12779528 | tf_op jit(solution)/shard_map/ppermute | solution.py:74
  47.0 97.1 %collective-permute-start.1 = (bf16[256,8320]{1,0:T(8,128)(2,1)}, bf16[256,8320]{1,0:T(8,128)(2,1)}, u32[]{:S(2)}, u32[]{:S(2)}) collective-permute-start(bf16[256,8320]{1,0:T(8,128)(2,1)} %concatenate.24), channel_id=1, source_target_pairs={{1,0},{2,3},{5,4},{6,7},{9,8},{10,11},{13,12},{14,15},{17,16},{18,... | collective-permute-start | bytes 12779528 | tf_op jit(solution)/shard_map/ppermute | solution.py:74
  130.2 104.1 %collective-permute-start.3 = (bf16[256,8320]{1,0:T(8,128)(2,1)}, bf16[256,8320]{1,0:T(8,128)(2,1)}, u32[]{:S(2)}, u32[]{:S(2)}) collective-permute-start(bf16[256,8320]{1,0:T(8,128)(2,1)} %collective-permute-done), channel_id=1, source_target_pairs={{1,0},{2,3},{5,4},{6,7},{9,8},{10,11},{13,12},{14,15},{17,16},{18,... | collective-permute-start | bytes 12779528 | tf_op jit(solution)/shard_map/ppermute | solution.py:74
  131.4 118.7 %all-to-all-start.1 = ((bf16[8,48,4096]{2,1,0:T(8,128)(2,1)}), bf16[8,48,4096]{2,1,0:T(8,128)(2,1)}, u32[]{:S(2)}, u32[]{:S(2)}) async-start(bf16[8,48,4096]{2,1,0:T(8,128)(2,1)} %bitcast.198), calls=%async_computation.1 | async-start | bytes 6291456 | tf_op jit(solution)/shard_map/all_to_all | solution.py:118
  152.3 91.0 %copy-start.47 = (f32[384]{0:T(512)S(1)}, f32[384]{0:T(512)}, u32[]{:S(2)}) copy-start(f32[384]{0:T(512)} %copy-done.46) | copy-start | bytes 4612
  250.2 77.5 %all-to-all-start.2 = ((bf16[8,48,8320]{2,1,0:T(8,128)(2,1)}), bf16[8,48,8320]{2,1,0:T(8,128)(2,1)}, u32[]{:S(2)}, u32[]{:S(2)}) async-start(bf16[8,48,8320]{2,1,0:T(8,128)(2,1)} %bitcast.193), calls=%async_computation.2 | async-start | bytes 12779520 | tf_op jit(solution)/shard_map/all_to_all | solution.py:118
  255.0 77.4 %collective-permute-start.9 = (bf16[256,8320]{1,0:T(8,128)(2,1)}, bf16[256,8320]{1,0:T(8,128)(2,1)}, u32[]{:S(2)}, u32[]{:S(2)}) collective-permute-start(bf16[256,8320]{1,0:T(8,128)(2,1)} %collective-permute-done.2), channel_id=1, source_target_pairs={{1,2},{2,1},{5,6},{6,5},{9,10},{10,9},{13,14},{14,13},{17,18},{18,... | collective-permute-start | bytes 12779528 | tf_op jit(solution)/shard_map/ppermute | solution.py:74
  327.6 77.4 %all-to-all-start.3 = ((bf16[8,48,8320]{2,1,0:T(8,128)(2,1)}), bf16[8,48,8320]{2,1,0:T(8,128)(2,1)}, u32[]{:S(2)}, u32[]{:S(2)}) async-start(bf16[8,48,8320]{2,1,0:T(8,128)(2,1)} %bitcast.192), calls=%async_computation.3 | async-start | bytes 12779520 | tf_op jit(solution)/shard_map/all_to_all | solution.py:118
  332.4 119.6 %collective-permute-start.10 = (bf16[256,8320]{1,0:T(8,128)(2,1)}, bf16[256,8320]{1,0:T(8,128)(2,1)}, u32[]{:S(2)}, u32[]{:S(2)}) collective-permute-start(bf16[256,8320]{1,0:T(8,128)(2,1)} %collective-permute-done.9), channel_id=1, source_target_pairs={{1,0},{2,3},{5,4},{6,7},{9,8},{10,11},{13,12},{14,15},{17,16},{18,... | collective-permute-start | bytes 12779528 | tf_op jit(solution)/shard_map/ppermute | solution.py:74
  405.1 42.5 %all-to-all-start.4 = ((bf16[8,48,4096]{2,1,0:T(8,128)(2,1)}), bf16[8,48,4096]{2,1,0:T(8,128)(2,1)}, u32[]{:S(2)}, u32[]{:S(2)}) async-start(bf16[8,48,4096]{2,1,0:T(8,128)(2,1)} %bitcast.200), calls=%async_computation.4 | async-start | bytes 6291456 | tf_op jit(solution)/shard_map/all_to_all | solution.py:118
  447.6 42.3 %all-to-all-start.5 = ((bf16[8,48,4096]{2,1,0:T(8,128)(2,1)}), bf16[8,48,4096]{2,1,0:T(8,128)(2,1)}, u32[]{:S(2)}, u32[]{:S(2)}) async-start(bf16[8,48,4096]{2,1,0:T(8,128)(2,1)} %bitcast.199), calls=%async_computation.5 | async-start | bytes 6291456 | tf_op jit(solution)/shard_map/all_to_all | solution.py:118
  489.9 77.6 %all-to-all-start.6 = ((bf16[8,48,8320]{2,1,0:T(8,128)(2,1)}), bf16[8,48,8320]{2,1,0:T(8,128)(2,1)}, u32[]{:S(2)}, u32[]{:S(2)}) async-start(bf16[8,48,8320]{2,1,0:T(8,128)(2,1)} %bitcast.190), calls=%async_computation.6 | async-start | bytes 12779520 | tf_op jit(solution)/shard_map/all_to_all | solution.py:118
  499.4 107.4 %collective-permute-start.4 = (bf16[256,4096]{1,0:T(8,128)(2,1)}, bf16[256,4096]{1,0:T(8,128)(2,1)}, u32[]{:S(2)}, u32[]{:S(2)}) collective-permute-start(bf16[256,4096]{1,0:T(8,128)(2,1)} %fusion.11), channel_id=1, source_target_pairs={{0,1},{3,2},{4,5},{7,6},{8,9},{11,10},{12,13},{15,14},{16,17},{19,... | collective-permute-start | bytes 6291464 | tf_op jit(solution)/shard_map/ppermute | solution.py:74
  508.3 83.6 %collective-permute-start.5 = (bf16[128,4096]{1,0:T(8,128)(2,1)}, bf16[128,4096]{1,0:T(8,128)(2,1)}, u32[]{:S(2)}, u32[]{:S(2)}) collective-permute-start(bf16[128,4096]{1,0:T(8,128)(2,1)} %get-tuple-element.75), channel_id=1, source_target_pairs={{0,1},{3,2},{4,5},{7,6},{8,9},{11,10},{12,13},{15,14},{16,17},{19,... | collective-permute-start | bytes 3145736 | tf_op jit(solution)/shard_map/ppermute | solution.py:74
  510.6 81.3 %collective-permute-start.7 = (bf16[128,4096]{1,0:T(8,128)(2,1)}, bf16[128,4096]{1,0:T(8,128)(2,1)}, u32[]{:S(2)}, u32[]{:S(2)}) collective-permute-start(bf16[128,4096]{1,0:T(8,128)(2,1)} %get-tuple-element.76), channel_id=1, source_target_pairs={{0,1},{3,2},{4,5},{7,6},{8,9},{11,10},{12,13},{15,14},{16,17},{19,... | collective-permute-start | bytes 3145736 | tf_op jit(solution)/shard_map/ppermute | solution.py:74
  587.3 42.4 %all-to-all-start.7 = ((bf16[8,48,4096]{2,1,0:T(8,128)(2,1)}), bf16[8,48,4096]{2,1,0:T(8,128)(2,1)}, u32[]{:S(2)}, u32[]{:S(2)}) async-start(bf16[8,48,4096]{2,1,0:T(8,128)(2,1)} %bitcast.29), calls=%async_computation.7 | async-start | bytes 6291456 | tf_op jit(solution)/shard_map/all_to_all | solution.py:118
  591.8 436.2 %all-gather.2.cloned.1.call-start = ((), (), s32[]{:S(2)}) async-start(), calls=%async_computation.10 | async-start | bytes 9437184 | tf_op jit(solution)/shard_map/all_gather | solution.py:261
  595.9 10.8 %collective-permute-start.8 = (bf16[128,4096]{1,0:T(8,128)(2,1)}, bf16[128,4096]{1,0:T(8,128)(2,1)}, u32[]{:S(2)}, u32[]{:S(2)}) collective-permute-start(bf16[128,4096]{1,0:T(8,128)(2,1)} %get-tuple-element.74), channel_id=1, source_target_pairs={{1,2},{2,1},{5,6},{6,5},{9,10},{10,9},{13,14},{14,13},{17,18},{18,... | collective-permute-start | bytes 3145736 | tf_op jit(solution)/shard_map/ppermute | solution.py:74
  597.8 9.0 collective-permute-start.6
  614.1 50.3 %copy-start.45 = (f32[256]{0:T(256)S(1)}, f32[256]{0:T(256)}, u32[]{:S(2)}) copy-start(f32[256]{0:T(256)} %copy-done.44) | copy-start | bytes 3076
  614.1 50.3 %copy-start.61 = (f32[256]{0:T(256)S(1)}, f32[256]{0:T(256)}, u32[]{:S(2)}) copy-start(f32[256]{0:T(256)} %get-tuple-element.97) | copy-start | bytes 3076
  629.7 34.7 %copy-start.2 = (f32[256,4096]{1,0:T(8,128)S(1)}, f32[256,4096]{1,0:T(8,128)}, u32[]{:S(2)}) copy-start(f32[256,4096]{1,0:T(8,128)} %get-tuple-element.108) | copy-start | bytes 12582916
  629.7 34.7 %copy-start.13 = (bf16[256,4096]{1,0:T(8,128)(2,1)S(1)}, bf16[256,4096]{1,0:T(8,128)(2,1)}, u32[]{:S(2)}) copy-start(bf16[256,4096]{1,0:T(8,128)(2,1)} %param.20) | copy-start | bytes 6291460
  633.3 39.4 %collective-permute-start.17 = (bf16[64,4096]{1,0:T(8,128)(2,1)S(1)}, bf16[64,4096]{1,0:T(8,128)(2,1)S(1)}, u32[]{:S(2)}, u32[]{:S(2)}) collective-permute-start(bf16[64,4096]{1,0:T(8,128)(2,1)S(1)} %get-tuple-element.69), channel_id=1, source_target_pairs={{0,1},{3,2},{4,5},{7,6},{8,9},{11,10},{12,13},{15,14},{16,17},{19,... | collective-permute-start | bytes 1572872 | tf_op jit(solution)/shard_map/ppermute | solution.py:74
  660.4 23.6 %collective-permute-start.11 = (bf16[64,4096]{1,0:T(8,128)(2,1)S(1)}, bf16[64,4096]{1,0:T(8,128)(2,1)S(1)}, u32[]{:S(2)}, u32[]{:S(2)}) collective-permute-start(bf16[64,4096]{1,0:T(8,128)(2,1)S(1)} %get-tuple-element.72), channel_id=1, source_target_pairs={{0,1},{3,2},{4,5},{7,6},{8,9},{11,10},{12,13},{15,14},{16,17},{19,... | collective-permute-start | bytes 1572872 | tf_op jit(solution)/shard_map/ppermute | solution.py:74
  661.7 33.5 %collective-permute-start.14 = (bf16[64,4096]{1,0:T(8,128)(2,1)S(1)}, bf16[64,4096]{1,0:T(8,128)(2,1)S(1)}, u32[]{:S(2)}, u32[]{:S(2)}) collective-permute-start(bf16[64,4096]{1,0:T(8,128)(2,1)S(1)} %get-tuple-element.71), channel_id=1, source_target_pairs={{0,1},{3,2},{4,5},{7,6},{8,9},{11,10},{12,13},{15,14},{16,17},{19,... | collective-permute-start | bytes 1572872 | tf_op jit(solution)/shard_map/ppermute | solution.py:74
  663.0 41.2 %collective-permute-start.20 = (bf16[64,4096]{1,0:T(8,128)(2,1)S(1)}, bf16[64,4096]{1,0:T(8,128)(2,1)S(1)}, u32[]{:S(2)}, u32[]{:S(2)}) collective-permute-start(bf16[64,4096]{1,0:T(8,128)(2,1)S(1)} %get-tuple-element.70), channel_id=1, source_target_pairs={{0,1},{3,2},{4,5},{7,6},{8,9},{11,10},{12,13},{15,14},{16,17},{19,... | collective-permute-start | bytes 1572872 | tf_op jit(solution)/shard_map/ppermute | solution.py:74
  667.7 40.1 %copy-start.58 = (f32[2,256]{1,0:T(2,128)S(1)}, f32[2,256]{1,0:T(2,128)}, u32[]{:S(2)}) copy-start(f32[2,256]{1,0:T(2,128)} %get-tuple-element.93) | copy-start | bytes 6148
  667.7 40.2 %copy-start.12 = (bf16[256,4096]{1,0:T(8,128)(2,1)S(1)}, bf16[256,4096]{1,0:T(8,128)(2,1)}, u32[]{:S(2)}) copy-start(bf16[256,4096]{1,0:T(8,128)(2,1)} %copy-done.11) | copy-start | bytes 6291460
  667.7 47.7 %collective-permute-start.23 = (bf16[256,4096]{1,0:T(8,128)(2,1)}, bf16[256,4096]{1,0:T(8,128)(2,1)}, u32[]{:S(2)}, u32[]{:S(2)}) collective-permute-start(bf16[256,4096]{1,0:T(8,128)(2,1)} %subtract_convert_fusion), channel_id=1, source_target_pairs={{1,2},{2,1},{5,6},{6,5},{9,10},{10,9},{13,14},{14,13},{17,18},{18,... | collective-permute-start | bytes 6291464 | tf_op jit(solution)/shard_map/ppermute | solution.py:74
  704.9 2.9 collective-permute-start.18
  705.6 2.2 collective-permute-start.21
  706.3 1.5 collective-permute-start.15
  707.0 0.8 collective-permute-start.12
  709.6 66.9 %collective-permute-start.22 = (bf16[64,4096]{1,0:T(8,128)(2,1)}, bf16[64,4096]{1,0:T(8,128)(2,1)S(1)}, u32[]{:S(2)}, u32[]{:S(2)}) collective-permute-start(bf16[64,4096]{1,0:T(8,128)(2,1)} %get-tuple-element.62), channel_id=1, source_target_pairs={{1,0},{2,3},{5,4},{6,7},{9,8},{10,11},{13,12},{14,15},{17,16},{18,... | collective-permute-start | bytes 1572872 | tf_op jit(solution)/shard_map/ppermute | solution.py:74
  710.9 76.9 %collective-permute-start.13 = (bf16[64,4096]{1,0:T(8,128)(2,1)}, bf16[64,4096]{1,0:T(8,128)(2,1)}, u32[]{:S(2)}, u32[]{:S(2)}) collective-permute-start(bf16[64,4096]{1,0:T(8,128)(2,1)} %get-tuple-element.64), channel_id=1, source_target_pairs={{1,0},{2,3},{5,4},{6,7},{9,8},{10,11},{13,12},{14,15},{17,16},{18,... | collective-permute-start | bytes 1572872 | tf_op jit(solution)/shard_map/ppermute | solution.py:74
  712.2 86.9 %collective-permute-start.16 = (bf16[64,4096]{1,0:T(8,128)(2,1)}, bf16[64,4096]{1,0:T(8,128)(2,1)}, u32[]{:S(2)}, u32[]{:S(2)}) collective-permute-start(bf16[64,4096]{1,0:T(8,128)(2,1)} %get-tuple-element.63), channel_id=1, source_target_pairs={{1,0},{2,3},{5,4},{6,7},{9,8},{10,11},{13,12},{14,15},{17,16},{18,... | collective-permute-start | bytes 1572872 | tf_op jit(solution)/shard_map/ppermute | solution.py:74
  713.5 96.7 %collective-permute-start.19 = (bf16[64,4096]{1,0:T(8,128)(2,1)}, bf16[64,4096]{1,0:T(8,128)(2,1)S(1)}, u32[]{:S(2)}, u32[]{:S(2)}) collective-permute-start(bf16[64,4096]{1,0:T(8,128)(2,1)} %get-tuple-element.61), channel_id=1, source_target_pairs={{1,0},{2,3},{5,4},{6,7},{9,8},{10,11},{13,12},{14,15},{17,16},{18,... | collective-permute-start | bytes 1572872 | tf_op jit(solution)/shard_map/ppermute | solution.py:74
  715.3 99.9 %copy-start.14 = (bf16[256,4096]{1,0:T(8,128)(2,1)S(1)}, bf16[256,4096]{1,0:T(8,128)(2,1)}, u32[]{:S(2)}) copy-start(bf16[256,4096]{1,0:T(8,128)(2,1)} %param.20) | copy-start | bytes 6291460
  715.3 331.4 %reduce-scatter.2.cloned.1.call-start = ((), (), s32[]{:S(2)}) async-start(), calls=%async_computation.11 | async-start | bytes 9437184 | tf_op jit(solution)/shard_map/reduce_scatter | solution.py:260
  715.3 99.8 %copy-start.3 = (f32[256,4096]{1,0:T(8,128)S(1)}, f32[256,4096]{1,0:T(8,128)}, u32[]{:S(2)}) copy-start(f32[256,4096]{1,0:T(8,128)} %get-tuple-element.108) | copy-start | bytes 12582916
  715.3 99.8 %copy-start.9 = (f32[256,4096]{1,0:T(8,128)S(1)}, f32[256,4096]{1,0:T(8,128)}, u32[]{:S(2)}) copy-start(f32[256,4096]{1,0:T(8,128)} %convert_element_type.291) | copy-start | bytes 12582916
  715.4 139.8 %collective-permute-start.24 = (bf16[256,4096]{1,0:T(8,128)(2,1)}, bf16[256,4096]{1,0:T(8,128)(2,1)S(1)}, u32[]{:S(2)}, u32[]{:S(2)}) collective-permute-start(bf16[256,4096]{1,0:T(8,128)(2,1)} %subtract_convert_fusion), channel_id=1, source_target_pairs={{1,0},{2,3},{5,4},{6,7},{9,8},{10,11},{13,12},{14,15},{17,16},{18,... | collective-permute-start | bytes 6291464 | tf_op jit(solution)/shard_map/ppermute | solution.py:74
  776.5 120.7 %collective-permute-start.25 = (bf16[256,4096]{1,0:T(8,128)(2,1)}, bf16[256,4096]{1,0:T(8,128)(2,1)S(1)}, u32[]{:S(2)}, u32[]{:S(2)}) collective-permute-start(bf16[256,4096]{1,0:T(8,128)(2,1)} %collective-permute-done.23), channel_id=1, source_target_pairs={{1,0},{2,3},{5,4},{6,7},{9,8},{10,11},{13,12},{14,15},{17,16},{18,... | collective-permute-start | bytes 6291464 | tf_op jit(solution)/shard_map/ppermute | solution.py:74
  816.7 42.5 %collective-permute-start.26 = (bf16[64,4096]{1,0:T(8,128)(2,1)S(1)}, bf16[64,4096]{1,0:T(8,128)(2,1)S(1)}, u32[]{:S(2)}, u32[]{:S(2)}) collective-permute-start(bf16[64,4096]{1,0:T(8,128)(2,1)S(1)} %get-tuple-element.60), channel_id=1, source_target_pairs={{0,1},{3,2},{4,5},{7,6},{8,9},{11,10},{12,13},{15,14},{16,17},{19,... | collective-permute-start | bytes 1572872 | tf_op jit(solution)/shard_map/ppermute | solution.py:74
  819.8 40.0 %collective-permute-start.27 = (bf16[64,4096]{1,0:T(8,128)(2,1)S(1)}, bf16[64,4096]{1,0:T(8,128)(2,1)S(1)}, u32[]{:S(2)}, u32[]{:S(2)}) collective-permute-start(bf16[64,4096]{1,0:T(8,128)(2,1)S(1)} %get-tuple-element.58), channel_id=1, source_target_pairs={{0,1},{3,2},{4,5},{7,6},{8,9},{11,10},{12,13},{15,14},{16,17},{19,... | collective-permute-start | bytes 1572872 | tf_op jit(solution)/shard_map/ppermute | solution.py:74
  821.6 37.6 %copy-start.23 = (bf16[64,4096]{1,0:T(8,128)(2,1)}, bf16[64,4096]{1,0:T(8,128)(2,1)S(1)}, u32[]{:S(2)}) copy-start(bf16[64,4096]{1,0:T(8,128)(2,1)S(1)} %get-tuple-element.56) | copy-start | bytes 1572868
  821.6 39.0 %collective-permute-start.28 = (bf16[64,4096]{1,0:T(8,128)(2,1)S(1)}, bf16[64,4096]{1,0:T(8,128)(2,1)S(1)}, u32[]{:S(2)}, u32[]{:S(2)}) collective-permute-start(bf16[64,4096]{1,0:T(8,128)(2,1)S(1)} %get-tuple-element.56), channel_id=1, source_target_pairs={{0,1},{3,2},{4,5},{7,6},{8,9},{11,10},{12,13},{15,14},{16,17},{19,... | collective-permute-start | bytes 1572872 | tf_op jit(solution)/shard_map/ppermute | solution.py:74
  855.2 8.2 collective-permute-start.29
  859.2 38.5 %collective-permute-start.30 = (bf16[64,4096]{1,0:T(8,128)(2,1)S(1)}, bf16[64,4096]{1,0:T(8,128)(2,1)S(1)}, u32[]{:S(2)}, u32[]{:S(2)}) collective-permute-start(bf16[64,4096]{1,0:T(8,128)(2,1)S(1)} %collective-permute-done.26), channel_id=1, source_target_pairs={{1,2},{2,1},{5,6},{6,5},{9,10},{10,9},{13,14},{14,13},{17,18},{18,... | collective-permute-start | bytes 1572872 | tf_op jit(solution)/shard_map/ppermute | solution.py:74
  859.9 39.4 %collective-permute-start.32 = (bf16[64,4096]{1,0:T(8,128)(2,1)S(1)}, bf16[64,4096]{1,0:T(8,128)(2,1)S(1)}, u32[]{:S(2)}, u32[]{:S(2)}) collective-permute-start(bf16[64,4096]{1,0:T(8,128)(2,1)S(1)} %collective-permute-done.27), channel_id=1, source_target_pairs={{1,2},{2,1},{5,6},{6,5},{9,10},{10,9},{13,14},{14,13},{17,18},{18,... | collective-permute-start | bytes 1572872 | tf_op jit(solution)/shard_map/ppermute | solution.py:74
  860.6 40.0 %collective-permute-start.34 = (bf16[64,4096]{1,0:T(8,128)(2,1)S(1)}, bf16[64,4096]{1,0:T(8,128)(2,1)S(1)}, u32[]{:S(2)}, u32[]{:S(2)}) collective-permute-start(bf16[64,4096]{1,0:T(8,128)(2,1)S(1)} %collective-permute-done.28), channel_id=1, source_target_pairs={{1,2},{2,1},{5,6},{6,5},{9,10},{10,9},{13,14},{14,13},{17,18},{18,... | collective-permute-start | bytes 1572872 | tf_op jit(solution)/shard_map/ppermute | solution.py:74
  863.4 38.5 %collective-permute-start.36 = (bf16[64,4096]{1,0:T(8,128)(2,1)S(1)}, bf16[64,4096]{1,0:T(8,128)(2,1)S(1)}, u32[]{:S(2)}, u32[]{:S(2)}) collective-permute-start(bf16[64,4096]{1,0:T(8,128)(2,1)S(1)} %collective-permute-done.29), channel_id=1, source_target_pairs={{1,2},{2,1},{5,6},{6,5},{9,10},{10,9},{13,14},{14,13},{17,18},{18,... | collective-permute-start | bytes 1572872 | tf_op jit(solution)/shard_map/ppermute | solution.py:74
  897.7 50.2 %copy-start.18 = (bf16[4,256,1024]{2,1,0:T(8,128)(2,1)S(1)}, bf16[4,256,1024]{2,1,0:T(8,128)(2,1)}, u32[]{:S(2)}) copy-start(bf16[4,256,1024]{2,1,0:T(8,128)(2,1)} %gather_fusion) | copy-start | bytes 6291460
  897.7 16.9 %collective-permute-start.31 = (bf16[64,4096]{1,0:T(8,128)(2,1)S(1)}, bf16[64,4096]{1,0:T(8,128)(2,1)S(1)}, u32[]{:S(2)}, u32[]{:S(2)}) collective-permute-start(bf16[64,4096]{1,0:T(8,128)(2,1)S(1)} %collective-permute-done.30), channel_id=1, source_target_pairs={{1,0},{2,3},{5,4},{6,7},{9,8},{10,11},{13,12},{14,15},{17,16},{18,... | collective-permute-start | bytes 1572872 | tf_op jit(solution)/shard_map/ppermute | solution.py:74
  899.3 26.5 %collective-permute-start.33 = (bf16[64,4096]{1,0:T(8,128)(2,1)S(1)}, bf16[64,4096]{1,0:T(8,128)(2,1)S(1)}, u32[]{:S(2)}, u32[]{:S(2)}) collective-permute-start(bf16[64,4096]{1,0:T(8,128)(2,1)S(1)} %collective-permute-done.32), channel_id=1, source_target_pairs={{1,0},{2,3},{5,4},{6,7},{9,8},{10,11},{13,12},{14,15},{17,16},{18,... | collective-permute-start | bytes 1572872 | tf_op jit(solution)/shard_map/ppermute | solution.py:74
  900.6 36.5 %collective-permute-start.35 = (bf16[64,4096]{1,0:T(8,128)(2,1)S(1)}, bf16[64,4096]{1,0:T(8,128)(2,1)S(1)}, u32[]{:S(2)}, u32[]{:S(2)}) collective-permute-start(bf16[64,4096]{1,0:T(8,128)(2,1)S(1)} %collective-permute-done.34), channel_id=1, source_target_pairs={{1,0},{2,3},{5,4},{6,7},{9,8},{10,11},{13,12},{14,15},{17,16},{18,... | collective-permute-start | bytes 1572872 | tf_op jit(solution)/shard_map/ppermute | solution.py:74
  901.9 42.6 %collective-permute-start.37 = (bf16[64,4096]{1,0:T(8,128)(2,1)S(1)}, bf16[64,4096]{1,0:T(8,128)(2,1)S(1)}, u32[]{:S(2)}, u32[]{:S(2)}) collective-permute-start(bf16[64,4096]{1,0:T(8,128)(2,1)S(1)} %collective-permute-done.36), channel_id=1, source_target_pairs={{1,0},{2,3},{5,4},{6,7},{9,8},{10,11},{13,12},{14,15},{17,16},{18,... | collective-permute-start | bytes 1572872 | tf_op jit(solution)/shard_map/ppermute | solution.py:74
  991.4 14.3 %all-to-all-start.8 = ((f32[32,1,48]{2,1,0:T(1,128)}), f32[32,1,48]{2,1,0:T(1,128)S(1)}, u32[]{:S(2)}, u32[]{:S(2)}) async-start(f32[32,1,48]{2,1,0:T(1,128)} %bitcast.50), calls=%async_computation.9 | async-start | bytes 32768 | tf_op jit(solution)/shard_map/all_to_all | solution.py:289
  1028.0 18.7 %copy-start.1 = (bf16[1,4096,384]{2,1,0:T(8,128)(2,1)S(1)}, bf16[1,4096,384]{2,1,0:T(8,128)(2,1)}, u32[]{:S(2)}) copy-start(bf16[1,4096,384]{2,1,0:T(8,128)(2,1)} %param.17) | copy-start | bytes 9437188
  (57 other events, 286.3 us)
Sparse Core Ops, SparseCore 0:
  715.4 105.8 all-gather.1
  959.3 69.5 reduce-scatter.1

commit v2 on v1

--- a/solution.py
+++ b/solution.py
@@ -87,9 +87,10 @@
     return hits[..., None, :] & (ranks[..., None, :] == slots[:, None])
 
 
-def expert_block(rows, cots, weights, gate_matrix, up_matrix, down_matrix):
-    gate_pre = jnp.dot(rows, gate_matrix, preferred_element_type=jnp.float32)
-    up_value = jnp.dot(rows, up_matrix, preferred_element_type=jnp.float32)
+def expert_block(rows, cots, weights, gate_up_matrix, down_matrix):
+    pre = jnp.dot(rows, gate_up_matrix, preferred_element_type=jnp.float32)
+    hidden = pre.shape[1] // 2
+    gate_pre, up_value = pre[:, :hidden], pre[:, hidden:]
     back_proj = lax.dot_general(cots, down_matrix, CONTRACT_LAST, preferred_element_type=jnp.float32)
     sigmoid_gate = jax.nn.sigmoid(gate_pre)
     silu_gate = gate_pre * sigmoid_gate
@@ -101,9 +102,10 @@
         act_grad * up_value * sigmoid_gate * (1.0 + gate_pre * (1.0 - sigmoid_gate))
     ).astype(jnp.bfloat16)
     up_grad = (act_grad * silu_gate).astype(jnp.bfloat16)
+    both_grads = jnp.concatenate([gate_grad, up_grad], axis=1)
     slot_grads = lax.dot_general(
-        gate_grad, gate_matrix, CONTRACT_LAST, preferred_element_type=jnp.float32
-    ) + lax.dot_general(up_grad, up_matrix, CONTRACT_LAST, preferred_element_type=jnp.float32)
+        both_grads, gate_up_matrix, CONTRACT_LAST, preferred_element_type=jnp.float32
+    )
     return (slot_grads.astype(jnp.bfloat16), weight_dots, weighted, gate_grad, up_grad)
 
 
@@ -137,7 +139,8 @@
     capacity = 3 * tok_rows * pick_count // (2 * experts)
     ctx_at, tp_at = lax.axis_index("ctx"), lax.axis_index("tp")
     arrival = jnp.array(ARRIVAL, jnp.int32)[tp_at]
-    gate_matrix, up_matrix, down_matrix = w_gate[0], w_up[0], w_down[0]
+    gate_up_matrix = jnp.concatenate([w_gate[0], w_up[0]], axis=1)
+    down_matrix = w_down[0]
 
     hidden_wide, rms_scale, normed = normalize(hidden_in, norm_gain)
     plane_experts = (jnp.arange(n_ctx) * (n_tp // 2) + tp_at // 2).astype(jnp.float32)
@@ -172,7 +175,7 @@
         pick_weights = slots[:, weight_at : weight_at + pick_count].astype(jnp.float32)
         weights = jnp.sum(jnp.where(named, pick_weights, 0.0), axis=1)
         slot_grads, weight_dots, weighted, gate_grad, up_grad = expert_block(
-            rows, cots, weights, gate_matrix, up_matrix, down_matrix
+            rows, cots, weights, gate_up_matrix, down_matrix
         )
         return (
             slot_grads.reshape(n_ctx, capacity, features),
@@ -188,6 +191,14 @@
             preferred_element_type=jnp.float32,
         ).astype(jnp.bfloat16)
 
+    def weight_grads(parts):
+        slots, weighted, gate_grad, up_grad = (jnp.concatenate(part, axis=0) for part in zip(*parts))
+        cots, rows = slots[:, :features], slots[:, features:id_at]
+        return tuple(
+            lax.dot_general(left, right, CONTRACT_FIRST, preferred_element_type=jnp.float32)
+            for left, right in ((weighted, cots), (rows, gate_grad), (rows, up_grad))
+        )
+
     from_end = hop(own_block, END_TO_MID)
     from_mid = hop(own_block, MID_TO_MID)
     near_mid = hop(own_block, MID_TO_END)
@@ -195,60 +206,92 @@
     slots0 = exchange(pack(choice0, own_block))
     grads0, dots0, kept0 = experts_on(slots0)
     back0 = exchange(grads0)
-    far_end = hop(after(from_end, grads0), MID_TO_MID)
-    far_mid = hop(after(from_mid, grads0), MID_TO_END)
+    from_end, from_mid, near_mid, _ = lax.optimization_barrier((from_end, from_mid, near_mid, grads0))
+    far_end = hop(from_end, MID_TO_MID)
+    far_mid = hop(from_mid, MID_TO_END)
     block1 = from_mid + near_mid
     choice1 = choose(block1)
     slots1 = exchange(after(pack(choice1, block1), back0))
     part0 = combine(choice0, back0)
-    last = hop(after(far_end, slots1), MID_TO_END)
+    grads1, dots1, kept1 = experts_on(after(slots1, part0))
+    back1 = exchange(grads1)
+    far_end, far_mid, _ = lax.optimization_barrier((far_end, far_mid, grads1))
+    last = hop(far_end, MID_TO_END)
     block2 = from_end + far_mid
     choice2 = choose(block2)
-    slots2 = exchange(after(pack(choice2, block2), slots1))
-    grads1, dots1, kept1 = experts_on(slots1)
-    back1 = exchange(after(grads1, slots2))
-    grads2, dots2, kept2 = experts_on(slots2)
-    back2 = exchange(after(grads2, back1))
-    block3 = far_end + last
+    slots2 = exchange(after(pack(choice2, block2), back1))
+    part1 = combine(choice1, back1)
+    from_near = hop(part1, END_TO_MID)
+    early = weight_grads([kept0, kept1])
+    grads2, dots2, kept2 = experts_on(after(slots2, from_near, *early))
+    back2 = exchange(grads2)
+    block3 = far_end + after(last, grads2)
     choice3 = choose(block3)
-    part1 = combine(choice1, back1)
     slots3 = exchange(after(pack(choice3, block3), back2))
     part2 = combine(choice2, back2)
-    grads3, dots3, kept3 = experts_on(slots3)
-    back3 = exchange(grads3)
-    part3 = combine(choice3, back3)
 
     def residual(total, at):
         return norm_backward(
             hidden_wide[at], rms_scale[at], norm_gain, total, grad_out[at]
         ).astype(jnp.bfloat16)
 
-    whole = slice(0, tok_rows)
-    halves = [slice(i * tok_rows // 2, (i + 1) * tok_rows // 2) for i in range(2)]
-    from_near = hop(part1, END_TO_MID)
-    from_far = []
-    for at in halves:
-        to_far = wide_sum(hop(part2[at], END_TO_MID), part1[at]).astype(jnp.bfloat16)
-        from_far.append(hop(to_far, MID_TO_MID))
-    mid_sum = wide_sum(part0, from_near, jnp.concatenate(from_far, axis=0))
-    mid_resid = residual(mid_sum, whole)
+    def plus(*terms):
+        return wide_sum(*terms).astype(jnp.bfloat16)
+
+    half_rows = tok_rows // 2
+    low, high = slice(0, half_rows), slice(half_rows, tok_rows)
+    first_half = hop(part2[low], END_TO_MID)
+    other_half = hop(after(part2, first_half)[high], END_TO_MID)
+    far_low = hop(plus(first_half, part1[low]), MID_TO_MID)
+    far_high = hop(plus(other_half, part1[high]), MID_TO_MID)
+    grads3, dots3, kept3 = experts_on(after(slots3, other_half))
+    back3 = exchange(grads3)
+    far_low, far_high, _ = lax.optimization_barrier((far_low, far_high, grads3))
+    mid_sum = wide_sum(part0, from_near, jnp.concatenate([far_low, far_high], axis=0))
+    mid_resid = residual(mid_sum, slice(0, tok_rows))
+    part3 = combine(choice3, back3)
     far_mid = hop(mid_resid, MID_TO_MID)
     near_mid = hop(mid_resid, MID_TO_END)
-    last_mid = hop(far_mid, MID_TO_END)
-    step = tok_rows // TOKEN_CHUNKS
-    own, second, third = [], [], []
-    for chunk in range(TOKEN_CHUNKS):
-        at = slice(chunk * step, (chunk + 1) * step)
-        passing = wide_sum(hop(part3[at], END_TO_MID), part3[at]).astype(jnp.bfloat16)
-        passing = wide_sum(hop(passing, MID_TO_MID), part2[at]).astype(jnp.bfloat16)
-        total = wide_sum(mid_sum[at], hop(passing, MID_TO_END))
-        resid = residual(total, at)
-        near_end = hop(resid, END_TO_MID)
-        far_end = hop(near_end, MID_TO_MID)
-        last_end = hop(far_end, MID_TO_END)
-        own.append(resid)
-        second.append(last_mid[at] + near_end)
-        third.append(far_end + last_end)
+
+    step_rows = tok_rows // TOKEN_CHUNKS
+    cuts = [slice(i * step_rows, (i + 1) * step_rows) for i in range(TOKEN_CHUNKS)]
+    at_hop = [[None] * TOKEN_CHUNKS for _ in range(6)]
+    own = [None] * TOKEN_CHUNKS
+    last_mid = [None] * TOKEN_CHUNKS
+    for step in range(TOKEN_CHUNKS + 5):
+        fresh = []
+        for place in range(6):
+            chunk = step - place
+            if not 0 <= chunk < TOKEN_CHUNKS:
+                continue
+            at = cuts[chunk]
+            came = at_hop[place - 1][chunk] if place else None
+            if place == 0:
+                sent = hop(part3[at], END_TO_MID)
+            elif place == 1:
+                sent = hop(plus(came, part3[at]), MID_TO_MID)
+            elif place == 2:
+                sent = hop(plus(came, part2[at]), MID_TO_END)
+            elif place == 3:
+                own[chunk] = residual(wide_sum(mid_sum[at], came), at)
+                sent = hop(own[chunk], END_TO_MID)
+            else:
+                sent = hop(came, MID_TO_MID if place == 4 else MID_TO_END)
+            at_hop[place][chunk] = sent
+            fresh.append((at_hop[place], chunk))
+        if 2 <= step < TOKEN_CHUNKS + 2:
+            last_mid[step - 2] = hop(far_mid[cuts[step - 2]], MID_TO_END)
+            fresh.append((last_mid, step - 2))
+        flying = [row[chunk] for row, chunk in fresh]
+        held = [part3, part2, mid_sum] + ([far_mid] if step else [])
+        landed = lax.optimization_barrier(tuple(flying + held))
+        part3, part2, mid_sum = landed[len(fresh) : len(fresh) + 3]
+        if step:
+            far_mid = landed[-1]
+        for (row, chunk), array in zip(fresh, landed):
+            row[chunk] = array
+    second = [left + right for left, right in zip(last_mid, at_hop[3])]
+    third = [left + right for left, right in zip(at_hop[4], at_hop[5])]
     resid_grad = jnp.concatenate(own, axis=0)
     columns = jnp.concatenate(own + [far_mid + near_mid] + second + third, axis=0)
 
@@ -269,17 +312,7 @@
         .reshape(n_tp * tok_rows, heads)
     )
 
-    def weight_grads(kept):
-        slots, weighted, gate_grad, up_grad = kept
-        cots, rows = slots[:, :features], slots[:, features:id_at]
-        return [
-            lax.dot_general(left, right, CONTRACT_FIRST, preferred_element_type=jnp.float32)
-            for left, right in ((weighted, cots), (rows, gate_grad), (rows, up_grad))
-        ]
-
-    early = [jnp.concatenate(parts, axis=0) for parts in zip(kept0, kept1, kept2)]
-    early = weight_grads([after(array, back2) for array in early])
-    late = weight_grads([after(array, weight_term) for array in kept3])
+    late = weight_grads([tuple(after(array, weight_term) for array in kept) for kept in (kept2, kept3)])
     down_wgrad, gate_wgrad, up_wgrad = (
         (first + then).astype(jnp.bfloat16) for first, then in zip(early, late)
     )

time: 1060 us -> 947 us (0.89)
  waiting for transfers between devices: 611 us -> 487 us
  starting transfers between devices: 127 us -> 149 us
  matrix products: 193 us -> 177 us
    ppermute x38 -> x41, waiting for transfers between devices: 324 us -> 239 us  [hop(): return lax.ppermute(array, 'tp', pairs)]
    all_to_all x8, waiting for transfers between devices: 287 us -> 231 us  [exchange(): return lax.all_to_all(array, 'ctx', split_axis=0, concat_axis=0, tiled=True)]
    ppermute x38 -> x41, starting transfers between devices: 86.1 us -> 108 us  [hop(): return lax.ppermute(array, 'tp', pairs)]
    unnamed x14 -> x13, other arithmetic: 6.98 us -> 21.7 us
    dot_general x16 -> x8, matrix products: 55 us -> 41.5 us  [the longest x4 25.4 us: expert_block(): pre = jnp.dot(rows, gate_up_matrix, preferred_element_type=jnp.float32)]
    concatenate x3 -> x0, other arithmetic: 13.5 us -> none  [per_device_line(): jnp.concatenate(parts, axis=0)]
  transfers between devices with their start and end apart: 49 -> 52, of which waited for: 24 -> 36; matrix products, arithmetic and copies ran while one was open for 24% -> 27% of each run, Pallas kernels for 0% -> 0%
where the time goes in v2:
time: 947 us; the launch traced here: 936 us
  waiting for transfers between devices  487 us (51%)
  matrix products  177 us (19%)
  starting transfers between devices  149 us (16%)
  other arithmetic  72.2 us (8%)
  local copies, waits for them, and re-layouts  35.2 us (4%)
  between operations  15.9 us (2%)
    ppermute x41, waiting for transfers between devices, hop(): return lax.ppermute(array, 'tp', pairs)  239 us
    all_to_all x8, waiting for transfers between devices, exchange(): return lax.all_to_all(array, 'ctx', split_axis=0, concat_axis=0, tiled=True)  231 us
    ppermute x41, starting transfers between devices, hop(): return lax.ppermute(array, 'tp', pairs)  108 us
    dot_general x6, matrix products, weight_grads(): lax.dot_general(left, right, CONTRACT_FIRST, preferred_element_type=jnp.f...  44.4 us
    all_to_all x8, starting transfers between devices, exchange(): return lax.all_to_all(array, 'ctx', split_axis=0, concat_axis=0, tiled=True)  37.6 us
    dot_general x4, matrix products, pack(): packed = jnp.dot(choice, block, preferred_element_type=jnp.float32)  26.8 us
    dot_general x4, matrix products, expert_block(): pre = jnp.dot(rows, gate_up_matrix, preferred_element_type=jnp.float32)  25.4 us
    unnamed x13, other arithmetic  21.7 us
  transfers between devices with their start and end apart: 52, of which 36 were waited for; matrix products, arithmetic and copies ran while one was open for 27% of the time, Pallas kernels for 0%

profile of v2, /device:TPU:0, one launch (start us, length us, event | category | flops | bytes accessed | tf_op | source)
XLA Modules:
  0.0 935.8 jit_solution(3115878911349533340)
XLA Ops:
  16.5 8.4 concatenate.51
  24.9 6.8 convolution_convert_fusion.3
  31.7 5.2 all-to-all-start
  36.9 6.6 collective-permute-start
  47.4 62.4 %all-to-all-done = bf16[8,48,8320]{2,1,0:T(8,128)(2,1)} async-done(((bf16[8,48,8320]{2,1,0:T(8,128)(2,1)}), bf16[8,48,8320]{2,1,0:T(8,128)(2,1)}, u32[]{:S(2)}, u32[]{:S(2)}) %all-to-all-start) | async-done | bytes 6389792 | tf_op jit(solution)/shard_map/all_to_all | solution.py:120
  110.9 6.3 fusion.35
  117.3 5.4 multiply_convert_fusion.12
  126.7 4.5 all-to-all-start.1
  133.5 8.7 collective-permute-done.2
  142.2 4.5 add.191
  149.1 6.7 convolution_convert_fusion.2
  155.8 13.3 %all-to-all-done.1 = bf16[8,48,4096]{2,1,0:T(8,128)(2,1)} async-done(((bf16[8,48,4096]{2,1,0:T(8,128)(2,1)}), bf16[8,48,4096]{2,1,0:T(8,128)(2,1)}, u32[]{:S(2)}, u32[]{:S(2)}) %all-to-all-start.1) | async-done | bytes 3145760 | tf_op jit(solution)/shard_map/all_to_all | solution.py:120
  169.1 5.0 all-to-all-start.2
  178.0 4.5 fusion.10
  182.5 64.2 %all-to-all-done.2 = bf16[8,48,8320]{2,1,0:T(8,128)(2,1)} async-done(((bf16[8,48,8320]{2,1,0:T(8,128)(2,1)}), bf16[8,48,8320]{2,1,0:T(8,128)(2,1)}, u32[]{:S(2)}, u32[]{:S(2)}) %all-to-all-start.2) | async-done | bytes 6389792 | tf_op jit(solution)/shard_map/all_to_all | solution.py:120
  247.9 6.3 fusion.31
  254.3 4.8 multiply_convert_fusion.10
  270.6 4.5 add.194
  277.6 6.7 convolution_convert_fusion.1
  284.2 21.3 %all-to-all-done.3 = bf16[8,48,4096]{2,1,0:T(8,128)(2,1)} async-done(((bf16[8,48,4096]{2,1,0:T(8,128)(2,1)}), bf16[8,48,4096]{2,1,0:T(8,128)(2,1)}, u32[]{:S(2)}, u32[]{:S(2)}) %all-to-all-start.3) | async-done | bytes 3145760 | tf_op jit(solution)/shard_map/all_to_all | solution.py:120
  305.5 4.7 all-to-all-start.4
  313.5 5.8 collective-permute-start.6
  320.9 8.9 fusion.43
  329.8 8.2 fusion.2
  338.0 9.0 fusion.44
  346.9 16.4 %collective-permute-done.6 = bf16[256,4096]{1,0:T(8,128)(2,1)} collective-permute-done((bf16[256,4096]{1,0:T(8,128)(2,1)S(1)}, bf16[256,4096]{1,0:T(8,128)(2,1)}, u32[]{:S(2)}, u32[]{:S(2)}) %collective-permute-start.6) | collective-permute-done | bytes 2097184 | tf_op jit(solution)/shard_map/ppermute | solution.py:74
  363.4 19.5 %all-to-all-done.4 = bf16[8,48,8320]{2,1,0:T(8,128)(2,1)} async-done(((bf16[8,48,8320]{2,1,0:T(8,128)(2,1)}), bf16[8,48,8320]{2,1,0:T(8,128)(2,1)}, u32[]{:S(2)}, u32[]{:S(2)}) %all-to-all-start.4) | async-done | bytes 6389792 | tf_op jit(solution)/shard_map/all_to_all | solution.py:120
  384.0 6.3 fusion.27
  390.4 5.2 multiply_convert_fusion.6
  404.1 11.4 %collective-permute-done.5 = bf16[256,8320]{1,0:T(8,128)(2,1)} collective-permute-done((bf16[256,8320]{1,0:T(8,128)(2,1)}, bf16[256,8320]{1,0:T(8,128)(2,1)}, u32[]{:S(2)}, u32[]{:S(2)}) %collective-permute-start.5) | collective-permute-done | bytes 4259872 | tf_op jit(solution)/shard_map/ppermute | solution.py:74
  415.5 4.5 add.197
  422.4 6.7 convolution_convert_fusion
  429.1 12.9 %all-to-all-done.5 = bf16[8,48,4096]{2,1,0:T(8,128)(2,1)} async-done(((bf16[8,48,4096]{2,1,0:T(8,128)(2,1)}), bf16[8,48,4096]{2,1,0:T(8,128)(2,1)}, u32[]{:S(2)}, u32[]{:S(2)}) %all-to-all-start.5) | async-done | bytes 3145760 | tf_op jit(solution)/shard_map/all_to_all | solution.py:120
  442.0 4.8 all-to-all-start.6
  454.6 22.9 %collective-permute-done.7 = bf16[128,4096]{1,0:T(8,128)(2,1)S(1)} collective-permute-done((bf16[128,4096]{1,0:T(8,128)(2,1)S(1)}, bf16[128,4096]{1,0:T(8,128)(2,1)S(1)}, u32[]{:S(2)}, u32[]{:S(2)}) %collective-permute-start.7) | collective-permute-done | bytes 1048608 | tf_op jit(solution)/shard_map/ppermute | solution.py:74
  482.1 22.2 %collective-permute-done.8 = bf16[128,4096]{1,0:T(8,128)(2,1)S(1)} collective-permute-done((bf16[128,4096]{1,0:T(8,128)(2,1)S(1)}, bf16[128,4096]{1,0:T(8,128)(2,1)S(1)}, u32[]{:S(2)}, u32[]{:S(2)}) %collective-permute-start.8) | collective-permute-done | bytes 1048608 | tf_op jit(solution)/shard_map/ppermute | solution.py:74
  509.8 9.6 %all-to-all-done.6 = bf16[8,48,8320]{2,1,0:T(8,128)(2,1)} async-done(((bf16[8,48,8320]{2,1,0:T(8,128)(2,1)}), bf16[8,48,8320]{2,1,0:T(8,128)(2,1)}, u32[]{:S(2)}, u32[]{:S(2)}) %all-to-all-start.6) | async-done | bytes 6389792 | tf_op jit(solution)/shard_map/all_to_all | solution.py:120
  519.4 6.3 fusion.23
  535.2 4.6 all-to-all-start.7
  549.5 28.2 %all-to-all-done.7 = bf16[8,48,4096]{2,1,0:T(8,128)(2,1)} async-done(((bf16[8,48,4096]{2,1,0:T(8,128)(2,1)}), bf16[8,48,4096]{2,1,0:T(8,128)(2,1)}, u32[]{:S(2)}, u32[]{:S(2)}) %all-to-all-start.7) | async-done | bytes 3145760 | tf_op jit(solution)/shard_map/all_to_all | solution.py:120
  581.0 4.5 collective-permute-start.9
  585.4 8.2 collective-permute-done.9
  598.9 6.5 collective-permute-done.12
  605.5 20.2 %collective-permute-start.15 = (bf16[64,4096]{1,0:T(8,128)(2,1)S(1)}, bf16[64,4096]{1,0:T(8,128)(2,1)S(1)}, u32[]{:S(2)}, u32[]{:S(2)}) collective-permute-start(bf16[64,4096]{1,0:T(8,128)(2,1)S(1)} %slice.251), channel_id=1, source_target_pairs={{0,1},{3,2},{4,5},{7,6},{8,9},{11,10},{12,13},{15,14},{16,17},{19,... | collective-permute-start | bytes 1572872 | tf_op jit(solution)/shard_map/ppermute | solution.py:74
  634.0 9.7 %collective-permute-done.17 = bf16[64,4096]{1,0:T(8,128)(2,1)S(1)} collective-permute-done((bf16[64,4096]{1,0:T(8,128)(2,1)S(1)}, bf16[64,4096]{1,0:T(8,128)(2,1)S(1)}, u32[]{:S(2)}, u32[]{:S(2)}) %collective-permute-start.17) | collective-permute-done | bytes 524320 | tf_op jit(solution)/shard_map/ppermute | solution.py:74
  643.7 6.9 collective-permute-done.18
  656.2 5.4 collective-permute-start.22
  670.9 5.3 collective-permute-done.23
  682.6 5.4 collective-permute-start.26
  695.5 8.6 collective-permute-done.28
  711.0 4.7 collective-permute-start.30
  723.6 9.8 %collective-permute-done.32 = bf16[64,4096]{1,0:T(8,128)(2,1)S(1)} collective-permute-done((bf16[64,4096]{1,0:T(8,128)(2,1)}, bf16[64,4096]{1,0:T(8,128)(2,1)S(1)}, u32[]{:S(2)}, u32[]{:S(2)}) %collective-permute-start.32) | collective-permute-done | bytes 524320 | tf_op jit(solution)/shard_map/ppermute | solution.py:74
  733.4 11.3 %collective-permute-done.33 = bf16[64,4096]{1,0:T(8,128)(2,1)} collective-permute-done((bf16[64,4096]{1,0:T(8,128)(2,1)S(1)}, bf16[64,4096]{1,0:T(8,128)(2,1)}, u32[]{:S(2)}, u32[]{:S(2)}) %collective-permute-start.33) | collective-permute-done | bytes 524320 | tf_op jit(solution)/shard_map/ppermute | solution.py:74
  749.7 4.9 collective-permute-done.34
  754.6 43.9 %collective-permute-done.36 = bf16[64,4096]{1,0:T(8,128)(2,1)S(1)} collective-permute-done((bf16[64,4096]{1,0:T(8,128)(2,1)S(1)}, bf16[64,4096]{1,0:T(8,128)(2,1)S(1)}, u32[]{:S(2)}, u32[]{:S(2)}) %collective-permute-start.36) | collective-permute-done | bytes 524320 | tf_op jit(solution)/shard_map/ppermute | solution.py:74
  801.3 12.1 %collective-permute-done.38 = bf16[64,4096]{1,0:T(8,128)(2,1)S(1)} collective-permute-done((bf16[64,4096]{1,0:T(8,128)(2,1)S(1)}, bf16[64,4096]{1,0:T(8,128)(2,1)S(1)}, u32[]{:S(2)}, u32[]{:S(2)}) %collective-permute-start.38) | collective-permute-done | bytes 524320 | tf_op jit(solution)/shard_map/ppermute | solution.py:74
  817.1 9.2 collective-permute-done.39
  843.9 14.5 %convolution_convert_fusion.4 = bf16[4096,1024]{1,0:T(8,128)(2,1)} fusion(bf16[1024,4096]{1,0:T(8,128)(2,1)} %add_dynamic-update-slice_fusion.1, bf16[1024,1024]{1,0:T(8,128)(2,1)S(1)} %bitcast.149), kind=kOutput, calls=%fused_computation.7 | convolution fusion | flops 8594128896 | bytes 18874368 | tf_op jit(solution)/shard_map/dot_general | solution.py:300
  864.4 7.0 all-to-all-done.8
  881.9 6.4 fusion.20
  888.3 7.1 fusion.14
  895.4 4.9 fusion.17
  900.4 14.9 %convolution_convert_fusion.9 = bf16[1024,1024]{1,0:T(8,128)(2,1)} fusion(bf16[1024,4096]{1,0:T(8,128)(2,1)} %add_dynamic-update-slice_fusion.1, bf16[4096,1024]{1,0:T(8,128)(2,1)} %all-gather.2.cloned.1.call-done), kind=kOutput, calls=%fused_computation.65 | convolution fusion | flops 8590983168 | bytes 18874368 | tf_op jit(solution)/shard_map/dot_general | solution.py:305
  918.8 9.7 %reduce-scatter.2.cloned.1.call-done = bf16[512,1024]{1,0:T(8,128)(2,1)} async-done(((bf16[4096,1024]{1,0:T(8,128)(2,1)}), bf16[512,1024]{1,0:T(8,128)(2,1)}) %reduce-scatter.2.cloned.1.call-update) | async-done | bytes 1048592 | tf_op jit(solution)/shard_map/reduce_scatter | solution.py:303
  (336 shorter events, 204.8 us)
Async XLA Ops:
  7.2 110.1 %copy-start = (bf16[1,384,4096]{2,1,0:T(8,128)(2,1)S(1)}, bf16[1,384,4096]{2,1,0:T(8,128)(2,1)}, u32[]{:S(2)}) copy-start(bf16[1,384,4096]{2,1,0:T(8,128)(2,1)} %param.19) | copy-start | bytes 9437188
  31.7 78.1 %all-to-all-start = ((bf16[8,48,8320]{2,1,0:T(8,128)(2,1)}), bf16[8,48,8320]{2,1,0:T(8,128)(2,1)}, u32[]{:S(2)}, u32[]{:S(2)}) async-start(bf16[8,48,8320]{2,1,0:T(8,128)(2,1)} %bitcast.142), calls=%async_computation | async-start | bytes 12779520 | tf_op jit(solution)/shard_map/all_to_all | solution.py:120
  36.9 96.6 %collective-permute-start = (bf16[256,8320]{1,0:T(8,128)(2,1)}, bf16[256,8320]{1,0:T(8,128)(2,1)}, u32[]{:S(2)}, u32[]{:S(2)}) collective-permute-start(bf16[256,8320]{1,0:T(8,128)(2,1)} %concatenate.51), channel_id=1, source_target_pairs={{0,1},{3,2},{4,5},{7,6},{8,9},{11,10},{12,13},{15,14},{16,17},{19,... | collective-permute-start | bytes 12779528 | tf_op jit(solution)/shard_map/ppermute | solution.py:74
  43.4 90.0 %collective-permute-start.1 = (bf16[256,8320]{1,0:T(8,128)(2,1)}, bf16[256,8320]{1,0:T(8,128)(2,1)}, u32[]{:S(2)}, u32[]{:S(2)}) collective-permute-start(bf16[256,8320]{1,0:T(8,128)(2,1)} %concatenate.51), channel_id=1, source_target_pairs={{1,2},{2,1},{5,6},{6,5},{9,10},{10,9},{13,14},{14,13},{17,18},{18,... | collective-permute-start | bytes 12779528 | tf_op jit(solution)/shard_map/ppermute | solution.py:74
  46.1 96.2 %collective-permute-start.2 = (bf16[256,8320]{1,0:T(8,128)(2,1)}, bf16[256,8320]{1,0:T(8,128)(2,1)}, u32[]{:S(2)}, u32[]{:S(2)}) collective-permute-start(bf16[256,8320]{1,0:T(8,128)(2,1)} %concatenate.51), channel_id=1, source_target_pairs={{1,0},{2,3},{5,4},{6,7},{9,8},{10,11},{13,12},{14,15},{17,16},{18,... | collective-permute-start | bytes 12779528 | tf_op jit(solution)/shard_map/ppermute | solution.py:74
  126.7 42.4 %all-to-all-start.1 = ((bf16[8,48,4096]{2,1,0:T(8,128)(2,1)}), bf16[8,48,4096]{2,1,0:T(8,128)(2,1)}, u32[]{:S(2)}, u32[]{:S(2)}) async-start(bf16[8,48,4096]{2,1,0:T(8,128)(2,1)} %bitcast.145), calls=%async_computation.1 | async-start | bytes 6291456 | tf_op jit(solution)/shard_map/all_to_all | solution.py:120
  169.1 77.6 %all-to-all-start.2 = ((bf16[8,48,8320]{2,1,0:T(8,128)(2,1)}), bf16[8,48,8320]{2,1,0:T(8,128)(2,1)}, u32[]{:S(2)}, u32[]{:S(2)}) async-start(bf16[8,48,8320]{2,1,0:T(8,128)(2,1)} %bitcast.143), calls=%async_computation.2 | async-start | bytes 12779520 | tf_op jit(solution)/shard_map/all_to_all | solution.py:120
  174.1 96.5 %collective-permute-start.4 = (bf16[256,8320]{1,0:T(8,128)(2,1)}, bf16[256,8320]{1,0:T(8,128)(2,1)}, u32[]{:S(2)}, u32[]{:S(2)}) collective-permute-start(bf16[256,8320]{1,0:T(8,128)(2,1)} %collective-permute-done.1), channel_id=1, source_target_pairs={{1,0},{2,3},{5,4},{6,7},{9,8},{10,11},{13,12},{14,15},{17,16},{18,... | collective-permute-start | bytes 12779528 | tf_op jit(solution)/shard_map/ppermute | solution.py:74
  175.4 92.2 %collective-permute-start.3 = (bf16[256,8320]{1,0:T(8,128)(2,1)}, bf16[256,8320]{1,0:T(8,128)(2,1)}, u32[]{:S(2)}, u32[]{:S(2)}) collective-permute-start(bf16[256,8320]{1,0:T(8,128)(2,1)} %collective-permute-done), channel_id=1, source_target_pairs={{1,2},{2,1},{5,6},{6,5},{9,10},{10,9},{13,14},{14,13},{17,18},{18,... | collective-permute-start | bytes 12779528 | tf_op jit(solution)/shard_map/ppermute | solution.py:74
  263.1 42.4 %all-to-all-start.3 = ((bf16[8,48,4096]{2,1,0:T(8,128)(2,1)}), bf16[8,48,4096]{2,1,0:T(8,128)(2,1)}, u32[]{:S(2)}, u32[]{:S(2)}) async-start(bf16[8,48,4096]{2,1,0:T(8,128)(2,1)} %bitcast.146), calls=%async_computation.3 | async-start | bytes 6291456 | tf_op jit(solution)/shard_map/all_to_all | solution.py:120
  305.5 77.4 %all-to-all-start.4 = ((bf16[8,48,8320]{2,1,0:T(8,128)(2,1)}), bf16[8,48,8320]{2,1,0:T(8,128)(2,1)}, u32[]{:S(2)}, u32[]{:S(2)}) async-start(bf16[8,48,8320]{2,1,0:T(8,128)(2,1)} %bitcast.141), calls=%async_computation.4 | async-start | bytes 12779520 | tf_op jit(solution)/shard_map/all_to_all | solution.py:120
  313.5 49.9 %collective-permute-start.6 = (bf16[256,4096]{1,0:T(8,128)(2,1)S(1)}, bf16[256,4096]{1,0:T(8,128)(2,1)}, u32[]{:S(2)}, u32[]{:S(2)}) collective-permute-start(bf16[256,4096]{1,0:T(8,128)(2,1)S(1)} %fusion.11), channel_id=1, source_target_pairs={{0,1},{3,2},{4,5},{7,6},{8,9},{11,10},{12,13},{15,14},{16,17},{19,... | collective-permute-start | bytes 6291464 | tf_op jit(solution)/shard_map/ppermute | solution.py:74
  319.3 96.1 %collective-permute-start.5 = (bf16[256,8320]{1,0:T(8,128)(2,1)}, bf16[256,8320]{1,0:T(8,128)(2,1)}, u32[]{:S(2)}, u32[]{:S(2)}) collective-permute-start(bf16[256,8320]{1,0:T(8,128)(2,1)} %collective-permute-done.3), channel_id=1, source_target_pairs={{1,0},{2,3},{5,4},{6,7},{9,8},{10,11},{13,12},{14,15},{17,16},{18,... | collective-permute-start | bytes 12779528 | tf_op jit(solution)/shard_map/ppermute | solution.py:74
  399.6 42.3 %all-to-all-start.5 = ((bf16[8,48,4096]{2,1,0:T(8,128)(2,1)}), bf16[8,48,4096]{2,1,0:T(8,128)(2,1)}, u32[]{:S(2)}, u32[]{:S(2)}) async-start(bf16[8,48,4096]{2,1,0:T(8,128)(2,1)} %bitcast.147), calls=%async_computation.5 | async-start | bytes 6291456 | tf_op jit(solution)/shard_map/all_to_all | solution.py:120
  442.0 77.4 %all-to-all-start.6 = ((bf16[8,48,8320]{2,1,0:T(8,128)(2,1)}), bf16[8,48,8320]{2,1,0:T(8,128)(2,1)}, u32[]{:S(2)}, u32[]{:S(2)}) async-start(bf16[8,48,8320]{2,1,0:T(8,128)(2,1)} %bitcast.140), calls=%async_computation.6 | async-start | bytes 12779520 | tf_op jit(solution)/shard_map/all_to_all | solution.py:120
  446.8 57.4 %copy-start.16 = (bf16[256,4096]{1,0:T(8,128)(2,1)S(1)}, bf16[256,4096]{1,0:T(8,128)(2,1)}, u32[]{:S(2)}) copy-start(bf16[256,4096]{1,0:T(8,128)(2,1)} %copy-done.15) | copy-start | bytes 6291460
  450.2 27.3 %collective-permute-start.7 = (bf16[128,4096]{1,0:T(8,128)(2,1)S(1)}, bf16[128,4096]{1,0:T(8,128)(2,1)S(1)}, u32[]{:S(2)}, u32[]{:S(2)}) collective-permute-start(bf16[128,4096]{1,0:T(8,128)(2,1)S(1)} %slice.311), channel_id=1, source_target_pairs={{0,1},{3,2},{4,5},{7,6},{8,9},{11,10},{12,13},{15,14},{16,17},{19,... | collective-permute-start | bytes 3145736 | tf_op jit(solution)/shard_map/ppermute | solution.py:74
  477.6 26.6 %collective-permute-start.8 = (bf16[128,4096]{1,0:T(8,128)(2,1)S(1)}, bf16[128,4096]{1,0:T(8,128)(2,1)S(1)}, u32[]{:S(2)}, u32[]{:S(2)}) collective-permute-start(bf16[128,4096]{1,0:T(8,128)(2,1)S(1)} %slice.239), channel_id=1, source_target_pairs={{0,1},{3,2},{4,5},{7,6},{8,9},{11,10},{12,13},{15,14},{16,17},{19,... | collective-permute-start | bytes 3145736 | tf_op jit(solution)/shard_map/ppermute | solution.py:74
  506.3 33.6 %collective-permute-start.10 = (bf16[128,4096]{1,0:T(8,128)(2,1)}, bf16[128,4096]{1,0:T(8,128)(2,1)}, u32[]{:S(2)}, u32[]{:S(2)}) collective-permute-start(bf16[128,4096]{1,0:T(8,128)(2,1)} %get-tuple-element.174), channel_id=1, source_target_pairs={{1,2},{2,1},{5,6},{6,5},{9,10},{10,9},{13,14},{14,13},{17,18},{18,... | collective-permute-start | bytes 3145736 | tf_op jit(solution)/shard_map/ppermute | solution.py:74
  508.0 31.9 %collective-permute-start.11 = (bf16[128,4096]{1,0:T(8,128)(2,1)}, bf16[128,4096]{1,0:T(8,128)(2,1)}, u32[]{:S(2)}, u32[]{:S(2)}) collective-permute-start(bf16[128,4096]{1,0:T(8,128)(2,1)} %get-tuple-element.173), channel_id=1, source_target_pairs={{1,2},{2,1},{5,6},{6,5},{9,10},{10,9},{13,14},{14,13},{17,18},{18,... | collective-permute-start | bytes 3145736 | tf_op jit(solution)/shard_map/ppermute | solution.py:74
  535.2 42.5 %all-to-all-start.7 = ((bf16[8,48,4096]{2,1,0:T(8,128)(2,1)}), bf16[8,48,4096]{2,1,0:T(8,128)(2,1)}, u32[]{:S(2)}, u32[]{:S(2)}) async-start(bf16[8,48,4096]{2,1,0:T(8,128)(2,1)} %bitcast.144), calls=%async_computation.7 | async-start | bytes 6291456 | tf_op jit(solution)/shard_map/all_to_all | solution.py:120
  539.8 360.5 %all-gather.2.cloned.1.call-start = ((), (), s32[]{:S(2)}) async-start(), calls=%async_computation.10 | async-start | bytes 9437184 | tf_op jit(solution)/shard_map/all_gather | solution.py:304
  547.5 51.4 %collective-permute-start.14 = (bf16[256,4096]{1,0:T(8,128)(2,1)}, bf16[256,4096]{1,0:T(8,128)(2,1)}, u32[]{:S(2)}, u32[]{:S(2)}) collective-permute-start(bf16[256,4096]{1,0:T(8,128)(2,1)} %subtract_convert_fusion), channel_id=1, source_target_pairs={{1,2},{2,1},{5,6},{6,5},{9,10},{10,9},{13,14},{14,13},{17,18},{18,... | collective-permute-start | bytes 6291464 | tf_op jit(solution)/shard_map/ppermute | solution.py:74
  580.9 45.7 %copy-start.9 = (bf16[256,4096]{1,0:T(8,128)(2,1)S(1)}, bf16[256,4096]{1,0:T(8,128)(2,1)}, u32[]{:S(2)}) copy-start(bf16[256,4096]{1,0:T(8,128)(2,1)} %copy-done.8) | copy-start | bytes 6291460
  581.0 12.7 %collective-permute-start.9 = (bf16[64,4096]{1,0:T(8,128)(2,1)S(1)}, bf16[64,4096]{1,0:T(8,128)(2,1)S(1)}, u32[]{:S(2)}, u32[]{:S(2)}) collective-permute-start(bf16[64,4096]{1,0:T(8,128)(2,1)S(1)} %slice.318), channel_id=1, source_target_pairs={{0,1},{3,2},{4,5},{7,6},{8,9},{11,10},{12,13},{15,14},{16,17},{19,... | collective-permute-start | bytes 1572872 | tf_op jit(solution)/shard_map/ppermute | solution.py:74
  593.6 11.8 %collective-permute-start.12 = (bf16[64,4096]{1,0:T(8,128)(2,1)S(1)}, bf16[64,4096]{1,0:T(8,128)(2,1)S(1)}, u32[]{:S(2)}, u32[]{:S(2)}) collective-permute-start(bf16[64,4096]{1,0:T(8,128)(2,1)S(1)} %slice.249), channel_id=1, source_target_pairs={{0,1},{3,2},{4,5},{7,6},{8,9},{11,10},{12,13},{15,14},{16,17},{19,... | collective-permute-start | bytes 1572872 | tf_op jit(solution)/shard_map/ppermute | solution.py:74
  598.2 7.2 collective-permute-start.13
  605.5 28.5 %collective-permute-start.15 = (bf16[64,4096]{1,0:T(8,128)(2,1)S(1)}, bf16[64,4096]{1,0:T(8,128)(2,1)S(1)}, u32[]{:S(2)}, u32[]{:S(2)}) collective-permute-start(bf16[64,4096]{1,0:T(8,128)(2,1)S(1)} %slice.251), channel_id=1, source_target_pairs={{0,1},{3,2},{4,5},{7,6},{8,9},{11,10},{12,13},{15,14},{16,17},{19,... | collective-permute-start | bytes 1572872 | tf_op jit(solution)/shard_map/ppermute | solution.py:74
  625.8 8.2 collective-permute-start.16
  626.8 16.9 %collective-permute-start.17 = (bf16[64,4096]{1,0:T(8,128)(2,1)S(1)}, bf16[64,4096]{1,0:T(8,128)(2,1)S(1)}, u32[]{:S(2)}, u32[]{:S(2)}) collective-permute-start(bf16[64,4096]{1,0:T(8,128)(2,1)S(1)} %add_convert_fusion.10), channel_id=1, source_target_pairs={{1,0},{2,3},{5,4},{6,7},{9,8},{10,11},{13,12},{14,15},{17,16},{18,... | collective-permute-start | bytes 1572872 | tf_op jit(solution)/shard_map/ppermute | solution.py:74
  629.3 21.3 %collective-permute-start.18 = (bf16[64,4096]{1,0:T(8,128)(2,1)S(1)}, bf16[64,4096]{1,0:T(8,128)(2,1)S(1)}, u32[]{:S(2)}, u32[]{:S(2)}) collective-permute-start(bf16[64,4096]{1,0:T(8,128)(2,1)S(1)} %slice.254), channel_id=1, source_target_pairs={{1,0},{2,3},{5,4},{6,7},{9,8},{10,11},{13,12},{14,15},{17,16},{18,... | collective-permute-start | bytes 1572872 | tf_op jit(solution)/shard_map/ppermute | solution.py:74
  631.1 50.1 %copy-start.6 = (f32[256,4096]{1,0:T(8,128)}, f32[256,4096]{1,0:T(8,128)S(1)}, u32[]{:S(2)}) copy-start(f32[256,4096]{1,0:T(8,128)S(1)} %convert_element_type.291) | copy-start | bytes 12582916
  651.0 13.0 %collective-permute-start.19 = (bf16[64,4096]{1,0:T(8,128)(2,1)S(1)}, bf16[64,4096]{1,0:T(8,128)(2,1)S(1)}, u32[]{:S(2)}, u32[]{:S(2)}) collective-permute-start(bf16[64,4096]{1,0:T(8,128)(2,1)S(1)} %slice.260), channel_id=1, source_target_pairs={{0,1},{3,2},{4,5},{7,6},{8,9},{11,10},{12,13},{15,14},{16,17},{19,... | collective-permute-start | bytes 1572872 | tf_op jit(solution)/shard_map/ppermute | solution.py:74
  652.8 11.2 %collective-permute-start.20 = (bf16[64,4096]{1,0:T(8,128)(2,1)S(1)}, bf16[64,4096]{1,0:T(8,128)(2,1)S(1)}, u32[]{:S(2)}, u32[]{:S(2)}) collective-permute-start(bf16[64,4096]{1,0:T(8,128)(2,1)S(1)} %add_convert_fusion.9), channel_id=1, source_target_pairs={{1,2},{2,1},{5,6},{6,5},{9,10},{10,9},{13,14},{14,13},{17,18},{18,... | collective-permute-start | bytes 1572872 | tf_op jit(solution)/shard_map/ppermute | solution.py:74
  653.7 14.1 %collective-permute-start.21 = (bf16[64,4096]{1,0:T(8,128)(2,1)S(1)}, bf16[64,4096]{1,0:T(8,128)(2,1)S(1)}, u32[]{:S(2)}, u32[]{:S(2)}) collective-permute-start(bf16[64,4096]{1,0:T(8,128)(2,1)S(1)} %add_convert_fusion.8), channel_id=1, source_target_pairs={{1,0},{2,3},{5,4},{6,7},{9,8},{10,11},{13,12},{14,15},{17,16},{18,... | collective-permute-start | bytes 1572872 | tf_op jit(solution)/shard_map/ppermute | solution.py:74
  656.2 14.7 %collective-permute-start.22 = (bf16[64,4096]{1,0:T(8,128)(2,1)S(1)}, bf16[64,4096]{1,0:T(8,128)(2,1)}, u32[]{:S(2)}, u32[]{:S(2)}) collective-permute-start(bf16[64,4096]{1,0:T(8,128)(2,1)S(1)} %get-tuple-element.170), channel_id=1, source_target_pairs={{0,1},{3,2},{4,5},{7,6},{8,9},{11,10},{12,13},{15,14},{16,17},{19,... | collective-permute-start | bytes 1572872 | tf_op jit(solution)/shard_map/ppermute | solution.py:74
  662.7 13.6 %collective-permute-start.23 = (bf16[64,4096]{1,0:T(8,128)(2,1)S(1)}, bf16[64,4096]{1,0:T(8,128)(2,1)S(1)}, u32[]{:S(2)}, u32[]{:S(2)}) collective-permute-start(bf16[64,4096]{1,0:T(8,128)(2,1)S(1)} %slice.263), channel_id=1, source_target_pairs={{1,0},{2,3},{5,4},{6,7},{9,8},{10,11},{13,12},{14,15},{17,16},{18,... | collective-permute-start | bytes 1572872 | tf_op jit(solution)/shard_map/ppermute | solution.py:74
  677.5 14.4 %collective-permute-start.24 = (bf16[64,4096]{1,0:T(8,128)(2,1)}, bf16[64,4096]{1,0:T(8,128)(2,1)}, u32[]{:S(2)}, u32[]{:S(2)}) collective-permute-start(bf16[64,4096]{1,0:T(8,128)(2,1)} %add_convert_fusion.7), channel_id=1, source_target_pairs={{1,2},{2,1},{5,6},{6,5},{9,10},{10,9},{13,14},{14,13},{17,18},{18,... | collective-permute-start | bytes 1572872 | tf_op jit(solution)/shard_map/ppermute | solution.py:74
  679.9 14.0 %collective-permute-start.25 = (bf16[64,4096]{1,0:T(8,128)(2,1)}, bf16[64,4096]{1,0:T(8,128)(2,1)S(1)}, u32[]{:S(2)}, u32[]{:S(2)}) collective-permute-start(bf16[64,4096]{1,0:T(8,128)(2,1)} %add_convert_fusion.6), channel_id=1, source_target_pairs={{1,0},{2,3},{5,4},{6,7},{9,8},{10,11},{13,12},{14,15},{17,16},{18,... | collective-permute-start | bytes 1572872 | tf_op jit(solution)/shard_map/ppermute | solution.py:74
  682.6 12.9 %collective-permute-start.26 = (bf16[64,4096]{1,0:T(8,128)(2,1)}, bf16[64,4096]{1,0:T(8,128)(2,1)}, u32[]{:S(2)}, u32[]{:S(2)}) collective-permute-start(bf16[64,4096]{1,0:T(8,128)(2,1)} %get-tuple-element.168), channel_id=1, source_target_pairs={{0,1},{3,2},{4,5},{7,6},{8,9},{11,10},{12,13},{15,14},{16,17},{19,... | collective-permute-start | bytes 1572872 | tf_op jit(solution)/shard_map/ppermute | solution.py:74
  688.0 7.5 collective-permute-start.27
  690.6 13.6 %collective-permute-start.28 = (bf16[64,4096]{1,0:T(8,128)(2,1)}, bf16[64,4096]{1,0:T(8,128)(2,1)}, u32[]{:S(2)}, u32[]{:S(2)}) collective-permute-start(bf16[64,4096]{1,0:T(8,128)(2,1)} %slice.271), channel_id=1, source_target_pairs={{1,0},{2,3},{5,4},{6,7},{9,8},{10,11},{13,12},{14,15},{17,16},{18,... | collective-permute-start | bytes 1572872 | tf_op jit(solution)/shard_map/ppermute | solution.py:74
  691.9 236.6 %reduce-scatter.2.cloned.1.call-start = ((), (), s32[]{:S(2)}) async-start(), calls=%async_computation.11 | async-start | bytes 9437184 | tf_op jit(solution)/shard_map/reduce_scatter | solution.py:303
  691.9 52.9 %copy-start.7 = (f32[256,4096]{1,0:T(8,128)S(1)}, f32[256,4096]{1,0:T(8,128)}, u32[]{:S(2)}) copy-start(f32[256,4096]{1,0:T(8,128)} %copy-done.6) | copy-start | bytes 12582916
  707.3 14.8 %collective-permute-start.29 = (bf16[64,4096]{1,0:T(8,128)(2,1)S(1)}, bf16[64,4096]{1,0:T(8,128)(2,1)S(1)}, u32[]{:S(2)}, u32[]{:S(2)}) collective-permute-start(bf16[64,4096]{1,0:T(8,128)(2,1)S(1)} %add_convert_fusion.5), channel_id=1, source_target_pairs={{1,0},{2,3},{5,4},{6,7},{9,8},{10,11},{13,12},{14,15},{17,16},{18,... | collective-permute-start | bytes 1572872 | tf_op jit(solution)/shard_map/ppermute | solution.py:74
  711.0 35.3 %copy-start.19 = (bf16[64,4096]{1,0:T(8,128)(2,1)}, bf16[64,4096]{1,0:T(8,128)(2,1)S(1)}, u32[]{:S(2)}) copy-start(bf16[64,4096]{1,0:T(8,128)(2,1)S(1)} %get-tuple-element.166) | copy-start | bytes 1572868
  711.0 103.7 %copy-start.57 = (s32[4,4]{1,0:T(4,128)S(1)}, s32[4,4]{1,0:T(4,128)}, u32[]{:S(2)}) copy-start(s32[4,4]{1,0:T(4,128)} %constant.61.clone) | copy-start | bytes 196
  711.0 12.6 %collective-permute-start.30 = (bf16[64,4096]{1,0:T(8,128)(2,1)S(1)}, bf16[64,4096]{1,0:T(8,128)(2,1)S(1)}, u32[]{:S(2)}, u32[]{:S(2)}) collective-permute-start(bf16[64,4096]{1,0:T(8,128)(2,1)S(1)} %get-tuple-element.166), channel_id=1, source_target_pairs={{0,1},{3,2},{4,5},{7,6},{8,9},{11,10},{12,13},{15,14},{16,17},{19,... | collective-permute-start | bytes 1572872 | tf_op jit(solution)/shard_map/ppermute | solution.py:74
  715.8 7.8 collective-permute-start.31
  716.5 17.0 %collective-permute-start.32 = (bf16[64,4096]{1,0:T(8,128)(2,1)}, bf16[64,4096]{1,0:T(8,128)(2,1)S(1)}, u32[]{:S(2)}, u32[]{:S(2)}) collective-permute-start(bf16[64,4096]{1,0:T(8,128)(2,1)} %copy-done.26), channel_id=1, source_target_pairs={{1,0},{2,3},{5,4},{6,7},{9,8},{10,11},{13,12},{14,15},{17,16},{18,... | collective-permute-start | bytes 1572872 | tf_op jit(solution)/shard_map/ppermute | solution.py:74
  718.8 25.9 %collective-permute-start.33 = (bf16[64,4096]{1,0:T(8,128)(2,1)S(1)}, bf16[64,4096]{1,0:T(8,128)(2,1)}, u32[]{:S(2)}, u32[]{:S(2)}) collective-permute-start(bf16[64,4096]{1,0:T(8,128)(2,1)S(1)} %slice.278), channel_id=1, source_target_pairs={{1,0},{2,3},{5,4},{6,7},{9,8},{10,11},{13,12},{14,15},{17,16},{18,... | collective-permute-start | bytes 1572872 | tf_op jit(solution)/shard_map/ppermute | solution.py:74
  722.1 104.1 %collective-permute-start.40 = (bf16[256,4096]{1,0:T(8,128)(2,1)}, bf16[256,4096]{1,0:T(8,128)(2,1)}, u32[]{:S(2)}, u32[]{:S(2)}) collective-permute-start(bf16[256,4096]{1,0:T(8,128)(2,1)} %subtract_convert_fusion), channel_id=1, source_target_pairs={{1,0},{2,3},{5,4},{6,7},{9,8},{10,11},{13,12},{14,15},{17,16},{18,... | collective-permute-start | bytes 6291464 | tf_op jit(solution)/shard_map/ppermute | solution.py:74
  723.6 74.9 %copy-start.30 = (bf16[64,4096]{1,0:T(8,128)(2,1)}, bf16[64,4096]{1,0:T(8,128)(2,1)S(1)}, u32[]{:S(2)}) copy-start(bf16[64,4096]{1,0:T(8,128)(2,1)S(1)} %collective-permute-done.30) | copy-start | bytes 1572868
  723.6 31.0 %copy-start.28 = (bf16[64,4096]{1,0:T(8,128)(2,1)}, bf16[64,4096]{1,0:T(8,128)(2,1)S(1)}, u32[]{:S(2)}) copy-start(bf16[64,4096]{1,0:T(8,128)(2,1)S(1)} %collective-permute-done.31) | copy-start | bytes 1572868
  746.3 8.2 collective-permute-start.34
  747.7 6.9 collective-permute-start.35
  748.4 50.1 %collective-permute-start.36 = (bf16[64,4096]{1,0:T(8,128)(2,1)S(1)}, bf16[64,4096]{1,0:T(8,128)(2,1)S(1)}, u32[]{:S(2)}, u32[]{:S(2)}) collective-permute-start(bf16[64,4096]{1,0:T(8,128)(2,1)S(1)} %collective-permute-done.31), channel_id=1, source_target_pairs={{1,0},{2,3},{5,4},{6,7},{9,8},{10,11},{13,12},{14,15},{17,16},{18,... | collective-permute-start | bytes 1572872 | tf_op jit(solution)/shard_map/ppermute | solution.py:74
  754.6 60.1 %copy-start.36 = (bf16[64,4096]{1,0:T(8,128)(2,1)}, bf16[64,4096]{1,0:T(8,128)(2,1)S(1)}, u32[]{:S(2)}) copy-start(bf16[64,4096]{1,0:T(8,128)(2,1)S(1)} %collective-permute-done.34) | copy-start | bytes 1572868
  754.6 60.2 %copy-start.34 = (bf16[64,4096]{1,0:T(8,128)(2,1)}, bf16[64,4096]{1,0:T(8,128)(2,1)S(1)}, u32[]{:S(2)}) copy-start(bf16[64,4096]{1,0:T(8,128)(2,1)S(1)} %collective-permute-done.35) | copy-start | bytes 1572868
  798.5 2.8 collective-permute-start.37
  800.0 13.4 %collective-permute-start.38 = (bf16[64,4096]{1,0:T(8,128)(2,1)S(1)}, bf16[64,4096]{1,0:T(8,128)(2,1)S(1)}, u32[]{:S(2)}, u32[]{:S(2)}) collective-permute-start(bf16[64,4096]{1,0:T(8,128)(2,1)S(1)} %collective-permute-done.35), channel_id=1, source_target_pairs={{1,0},{2,3},{5,4},{6,7},{9,8},{10,11},{13,12},{14,15},{17,16},{18,... | collective-permute-start | bytes 1572872 | tf_op jit(solution)/shard_map/ppermute | solution.py:74
  813.4 12.8 %collective-permute-start.39 = (bf16[64,4096]{1,0:T(8,128)(2,1)}, bf16[64,4096]{1,0:T(8,128)(2,1)}, u32[]{:S(2)}, u32[]{:S(2)}) collective-permute-start(bf16[64,4096]{1,0:T(8,128)(2,1)} %collective-permute-done.37), channel_id=1, source_target_pairs={{1,0},{2,3},{5,4},{6,7},{9,8},{10,11},{13,12},{14,15},{17,16},{18,... | collective-permute-start | bytes 1572872 | tf_op jit(solution)/shard_map/ppermute | solution.py:74
  860.8 10.6 %all-to-all-start.8 = ((f32[32,1,48]{2,1,0:T(1,128)}), f32[32,1,48]{2,1,0:T(1,128)S(1)}, u32[]{:S(2)}, u32[]{:S(2)}) async-start(f32[32,1,48]{2,1,0:T(1,128)} %bitcast.50), calls=%async_computation.9 | async-start | bytes 32768 | tf_op jit(solution)/shard_map/all_to_all | solution.py:322
  900.4 28.2 %copy-start.1 = (bf16[1,384,4096]{2,1,0:T(8,128)(2,1)S(1)}, bf16[1,384,4096]{2,1,0:T(8,128)(2,1)}, u32[]{:S(2)}) copy-start(bf16[1,384,4096]{2,1,0:T(8,128)(2,1)} %param.19) | copy-start | bytes 9437188
  (66 other events, 552.6 us)
Sparse Core Ops, SparseCore 0:
  692.0 55.3 all-gather.1
  858.6 69.8 reduce-scatter.1
